TPU v7x, 512 devices: a whole 4x8x8 slice. The times are simulated.
512 devices in a mesh: rows: 32 (over x, z), cols: 16 (over y, core).
Axes of the slice: x: 4, y: 8, z: 8, core: 2. Of those that a mesh axis runs over, the one named last changes fastest.
Arguments:
- matrix: float32 [65536, 4096], P('rows', 'cols'), may hold values from -80 to 80
- gaussian: float32 [256, 65536], P(None, 'rows'), may hold values from -0.046875 to 0.046875
- pivots: int32 [256], replicated, may hold values from 0 to 4095, as said below
- trailing: float32 [65536, 512], P('rows', 'cols'), may hold values from -6 to 6
Outputs:
- sketch: float32 [256, 4096], P('rows', 'cols')
- coupling: float32 [256, 512], P(None, 'cols')
- projected: float32 [65536, 512], P('rows', 'cols')
- trailing_sketch: float32 [256, 512], P('rows', 'cols')
Inputs may be any that keep to these rules, and one draw needn't show every extreme that they name: `pivots`: 256 distinct column indices; at most 64 of them lie in one block of 256 consecutive columns starting at a multiple of 256, and exactly 64 in some such block.
All inputs are finite; a program needn't handle non-finite values.
Results may differ from a plain program's by a relative error of at most 0.00015.
Values sent between devices are 32-bit elements; how exact they have to be, the bound alone decides.
No kernel may reach another device: no remote copies, remote signals or barrier semaphores. Data moves between devices by JAX's collectives and lax.ppermute only.
A program may use at most 64 MiB of HBM per device.

v0:
```python
import jax
import jax.numpy as jnp
from jax import lax
from jax.sharding import PartitionSpec as P


def inner_rows(left, right):
    return lax.dot_general(
        left,
        right,
        (((0,), (0,)), ((), ())),
        precision=lax.Precision.HIGHEST,
        preferred_element_type=jnp.float32,
    )


def product(left, right):
    return jnp.dot(left, right, precision=lax.Precision.HIGHEST, preferred_element_type=jnp.float32)


def factor_parts(gram_matrix, cross_terms):
    chol_factor = jnp.linalg.cholesky(gram_matrix)
    coupling = lax.linalg.triangular_solve(chol_factor, cross_terms, left_side=True, lower=True)
    weights = lax.linalg.triangular_solve(
        chol_factor, coupling, left_side=True, lower=True, transpose_a=True
    )
    return (coupling, weights)


def shards(matrix, gaussian, pivots, trailing):
    rows_dev, cols_dev = matrix.shape
    sketch_rows = gaussian.shape[0]
    panel_width = pivots.shape[0]
    row_groups = lax.axis_size("rows")
    sketch_share = sketch_rows // row_groups
    row_start = lax.axis_index("rows") * sketch_share
    col_block = lax.axis_index("cols")
    sketch = lax.psum_scatter(product(gaussian, matrix), "rows", scatter_dimension=0, tiled=True)
    local_index = pivots - col_block * cols_dev
    selector = (
        lax.broadcasted_iota(jnp.int32, (cols_dev, panel_width), 0) == local_index[None, :]
    ).astype(jnp.float32)
    panel_block = lax.psum(product(matrix, selector), "cols")
    gram_matrix, cross_terms, gauss_panel, gauss_trail = lax.psum(
        (
            inner_rows(panel_block, panel_block),
            inner_rows(panel_block, trailing),
            product(gaussian, panel_block),
            product(gaussian, trailing),
        ),
        "rows",
    )
    coupling, weights = factor_parts(gram_matrix, cross_terms)
    projected = trailing - product(panel_block, weights)
    sketch_full = gauss_trail - product(gauss_panel, weights)
    trailing_sketch = lax.dynamic_slice_in_dim(sketch_full, row_start, sketch_share, 0)
    return (sketch, coupling, projected, trailing_sketch)


def solution(mesh):
    placed = (P("rows", "cols"), P(None, "rows"), P(), P("rows", "cols"))
    return jax.shard_map(
        shards,
        mesh=mesh,
        in_specs=placed,
        out_specs=(P("rows", "cols"), P(None, "cols"), P("rows", "cols"), P("rows", "cols")),
        check_vma=False,
    )
```

profile of v0, /device:TPU:1, one launch (start us, length us, event | category | flops | bytes accessed | tf_op | source)
XLA Modules:
  0.0 683.5 jit_solution(2420182431590510024)
XLA Ops:
  7.2 0.0 copy-start
  7.2 0.0 all-reduce.7.cloned.1.call-start
  7.2 0.8 broadcast_subtract_fusion
  8.1 0.7 copy-done
  8.8 2.6 convolution_bitcast_fusion
  11.4 0.0 all-reduce.7.cloned.1.call-update
  11.4 0.0 all-reduce.11.cloned.1.call-start
  11.4 125.5 %all-reduce.7.cloned.1.call-done = f32[2048,256]{0,1:T(8,128)} async-done(((f32[2048,256]{0,1:T(8,128)}), f32[2048,256]{0,1:T(8,128)}) %all-reduce.7.cloned.1.call-update) | async-done | bytes 2097168 | tf_op jit(solution)/shard_map/psum | solution.py:43
  137.0 4.9 fusion.19
  141.9 2.6 convolution_bitcast_fusion.1
  144.5 0.0 all-reduce.11.cloned.1.call-update
  144.5 0.0 all-reduce.9.cloned.1.call-start
  144.6 4.2 fusion.21
  148.8 0.0 copy-done.2
  148.8 2.5 fusion.20
  151.3 0.0 all-reduce.9.cloned.1.call-update
  151.3 0.2 reduce-scatter.2.cloned.1.call-start
  151.5 4.2 fusion.18
  155.7 0.0 reduce-scatter.2.cloned.1.call-update
  155.8 144.6 %all-reduce.11.cloned.1.call-done = (f32[256,256]{0,1:T(8,128)}, f32[256,256]{0,1:T(8,128)}) async-done(((f32[256,256]{0,1:T(8,128)}, f32[256,256]{0,1:T(8,128)}), (f32[256,256]{0,1:T(8,128)}, f32[256,256]{0,1:T(8,128)})) %all-reduce.11.cloned.1.call-update) | async-done | bytes 524304 | tf_op jit(solution)/shard_map/psum | solution.py:44
  300.4 1.1 copy.9
  301.4 1.0 fusion
  302.5 11.7 %cholesky.50 = f32[128,128]{1,0:T(8,128)S(1)} custom-call(f32[128,128]{1,0:T(8,128)S(1)} %cholesky.118), custom_call_target="Cholesky" | custom-call | tf_op jit(solution)/shard_map/jit(cholesky)/cholesky | solution.py:22
  314.2 9.8 %custom-call.16 = f32[1,128,128]{1,2,0:T(8,128)S(1)} custom-call(f32[1,128,128]{2,1,0:T(8,128)S(1)} %get-tuple-element.29), custom_call_target="InvertDiagBlocksLowerTriangular" | custom-call | tf_op jit(solution)/shard_map/jit(cholesky)/cholesky | solution.py:22
  324.1 0.2 constant_dynamic-update-slice_fusion
  324.3 0.3 convolution_subtract_fusion.1
  324.6 11.8 %cholesky.105 = f32[128,128]{1,0:T(8,128)S(1)} custom-call(f32[128,128]{1,0:T(8,128)S(1)} %convolution_subtract_fusion.1), custom_call_target="Cholesky" | custom-call | tf_op jit(solution)/shard_map/jit(cholesky)/cholesky | solution.py:22
  336.4 0.7 compare_reduce_fusion
  338.5 0.1 triangular_solve.68
  338.5 4.1 while.1
  338.6 0.6 fusion.43
  339.1 1.4 bitcast_dynamic-update-slice_fusion.2
  340.6 0.6 fusion.43
  341.2 1.4 bitcast_dynamic-update-slice_fusion.2
  342.6 19.7 %custom-call.17 = f32[2,128,128]{1,2,0:T(8,128)S(1)} custom-call(f32[2,128,128]{2,1,0:T(8,128)S(1)} %get-tuple-element.11), custom_call_target="InvertDiagBlocksLowerTriangular" | custom-call | tf_op jit(solution)/shard_map/triangular_solve | solution.py:23
  362.3 93.2 %all-reduce.9.cloned.1.call-done = (f32[256,32]{0,1:T(8,128)}, f32[256,32]{1,0:T(8,128)}) async-done(((f32[256,32]{0,1:T(8,128)}, f32[256,32]{1,0:T(8,128)}), (f32[256,32]{0,1:T(8,128)}, f32[256,32]{1,0:T(8,128)})) %all-reduce.9.cloned.1.call-update) | async-done | bytes 65552 | tf_op jit(solution)/shard_map/psum | solution.py:44
  455.5 0.9 fusion.8
  456.4 0.9 convolution_subtract_fusion.3
  457.3 0.2 fusion.10
  457.5 0.2 fusion.9
  457.7 0.2 convolution_subtract_fusion.2
  457.9 0.2 fusion.7
  458.1 0.0 copy-done.5
  458.1 0.6 fusion.13
  458.7 1.3 dynamic-slice_subtract_fusion
  460.0 0.6 pad_maximum_fusion
  460.6 3.6 convolution_subtract_fusion
  464.3 212.7 %reduce-scatter.2.cloned.1.call-done = f32[8,256]{1,0:T(8,128)} async-done(((f32[256,256]{1,0:T(8,128)}), f32[8,256]{1,0:T(8,128)}) %reduce-scatter.2.cloned.1.call-update) | async-done | bytes 8208 | tf_op jit(solution)/shard_map/reduce_scatter | solution.py:38
  (17 shorter events, 0.2 us)
Async XLA Ops:
  7.2 1.6 copy-start
  7.2 129.8 %all-reduce.7.cloned.1.call-start = ((), (), s32[]{:S(2)}) async-start(), calls=%async_computation.2 | async-start | bytes 4194304 | tf_op jit(solution)/shard_map/psum | solution.py:43
  11.4 289.0 %all-reduce.11.cloned.1.call-start = ((), (), s32[]{:S(2)}) async-start(), calls=%async_computation.4 | async-start | bytes 1048576 | tf_op jit(solution)/shard_map/psum | solution.py:44
  137.0 4.9 copy-start.1
  137.0 4.9 copy-start.3
  141.9 2.7 copy-start.4
  144.5 311.0 %all-reduce.9.cloned.1.call-start = ((), (), s32[]{:S(2)}) async-start(), calls=%async_computation.3 | async-start | bytes 327680 | tf_op jit(solution)/shard_map/psum | solution.py:44
  144.6 4.2 copy-start.2
  151.3 525.6 %reduce-scatter.2.cloned.1.call-start = ((), (), s32[]{:S(2)}) async-start(), calls=%async_computation.1 | async-start | bytes 270336 | tf_op jit(solution)/shard_map/reduce_scatter | solution.py:38
  301.4 156.7 %copy-start.5 = (f32[256,256]{0,1:T(8,128)S(1)}, f32[256,256]{0,1:T(8,128)}, u32[]{:S(2)}) copy-start(f32[256,256]{0,1:T(8,128)} %get-tuple-element.23) | copy-start | bytes 786436
Sparse Core Ops, SparseCore 0:
  11.5 125.4 all-reduce.6
  144.7 155.6 all-reduce.10
  304.9 150.5 all-reduce.8
  460.3 216.5 reduce-scatter.1
where the time goes:
time: 688 us; the launch traced here: 683 us
  waiting for transfers between devices  576 us (84%)
  other arithmetic  57.5 us (8%)
  matrix products  28.2 us (4%)
  between operations  15.3 us (2%)
    psum x2, waiting for transfers between devices, shards(): lax.psum((inner_rows(panel_block, panel_block), inner_rows(panel_block, t...  238 us
    reduce_scatter x1, waiting for transfers between devices, shards(): lax.psum_scatter(product(gaussian, matrix), 'rows', scatter_dimension=0,...  213 us
    psum x1, waiting for transfers between devices, shards(): panel_block = lax.psum(product(matrix, selector), 'cols')  126 us
    another operation x6, other arithmetic, factor_parts(): chol_factor = jnp.linalg.cholesky(gram_matrix)  34.1 us
    another operation x4, other arithmetic, factor_parts(): lax.linalg.triangular_solve(chol_factor, cross_terms, left_side=True, low...  20.3 us
    dot_general x6, matrix products, product(): jnp.dot(left, right, precision=lax.Precision.HIGHEST, preferred_element_t...  17.7 us
  transfers between devices with their start and end apart: 4, of which 4 were waited for; matrix products, arithmetic and copies ran while one was open for 12% of the time, Pallas kernels for 0%

commit v1 on v0

v1 whole, which is shorter than its diff:
```python
import jax
import jax.numpy as jnp
from jax import lax
from jax.sharding import PartitionSpec as P

MOST = 64


def inner_rows(left, right):
    return lax.dot_general(
        left,
        right,
        (((0,), (0,)), ((), ())),
        precision=lax.Precision.HIGHEST,
        preferred_element_type=jnp.float32,
    )


def product(left, right):
    return jnp.dot(left, right, precision=lax.Precision.HIGHEST, preferred_element_type=jnp.float32)


def factor_parts(gram_matrix, cross_terms):
    chol_factor = jnp.linalg.cholesky(gram_matrix)
    coupling = lax.linalg.triangular_solve(chol_factor, cross_terms, left_side=True, lower=True)
    weights = lax.linalg.triangular_solve(
        chol_factor, coupling, left_side=True, lower=True, transpose_a=True
    )
    return (coupling, weights)


def scatter_sum(partial, axis):
    n = lax.axis_size(axis)
    pieces = partial.reshape((n, partial.shape[0] // n) + partial.shape[1:])
    return jnp.sum(lax.all_to_all(pieces, axis, 0, 0, tiled=True), axis=0)


def gather_blocks(block, axis):
    n = lax.axis_size(axis)
    copies = jnp.broadcast_to(block[None], (n,) + block.shape)
    got = lax.all_to_all(copies, axis, 0, 0, tiled=True)
    return got.reshape((n * block.shape[0],) + block.shape[1:])


def shards(matrix, gaussian, pivots, trailing):
    rows_dev, cols_dev = matrix.shape
    panel_width = pivots.shape[0]
    col_groups = lax.axis_size("cols")
    col_block = lax.axis_index("cols")
    owner = pivots // cols_dev
    earlier = jnp.arange(panel_width)[None, :] < jnp.arange(panel_width)[:, None]
    slot = jnp.sum((owner[None, :] == owner[:, None]) & earlier, axis=1, dtype=jnp.int32)
    local_index = pivots - col_block * cols_dev
    column_hot = (
        lax.broadcasted_iota(jnp.int32, (cols_dev, panel_width), 0) == local_index[None, :]
    ).astype(jnp.bfloat16)
    slot_hot = (
        lax.broadcasted_iota(jnp.int32, (panel_width, MOST), 1) == slot[:, None]
    ).astype(jnp.bfloat16)
    pick = jnp.dot(column_hot, slot_hot, preferred_element_type=jnp.float32)
    mine = product(matrix, pick)
    spread = lax.all_to_all(
        mine.reshape(col_groups, rows_dev // col_groups, MOST), "cols", 0, 0, tiled=True
    )
    place = (
        lax.broadcasted_iota(jnp.int32, (col_groups * MOST, panel_width), 0)
        == (owner * MOST + slot)[None, :]
    ).astype(jnp.float32)
    part = lax.dot_general(
        spread,
        place.reshape(col_groups, MOST, panel_width),
        (((0, 2), (0, 1)), ((), ())),
        precision=lax.Precision.HIGHEST,
        preferred_element_type=jnp.float32,
    )
    panel_block = lax.all_gather(part, "cols", tiled=True)

    sketch_part = jnp.concatenate([product(gaussian, matrix), product(gaussian, trailing)], axis=1)
    sketch_rows = scatter_sum(sketch_part, "rows")
    sketch = sketch_rows[:, :cols_dev]
    gauss_trail = sketch_rows[:, cols_dev:]

    sums = scatter_sum(
        jnp.concatenate(
            [
                inner_rows(panel_block, panel_block),
                product(gaussian, panel_block),
                inner_rows(panel_block, trailing),
            ],
            axis=1,
        ),
        "rows",
    )
    gauss_panel = sums[:, panel_width : 2 * panel_width]
    whole = gather_blocks(
        jnp.concatenate([sums[:, :panel_width], sums[:, 2 * panel_width :]], axis=1), "rows"
    )
    coupling, weights = factor_parts(whole[:, :panel_width], whole[:, panel_width:])
    projected = trailing - product(panel_block, weights)
    trailing_sketch = gauss_trail - product(gauss_panel, weights)
    return (sketch, coupling, projected, trailing_sketch)


def solution(mesh):
    placed = (P("rows", "cols"), P(None, "rows"), P(), P("rows", "cols"))
    return jax.shard_map(
        shards,
        mesh=mesh,
        in_specs=placed,
        out_specs=(P("rows", "cols"), P(None, "cols"), P("rows", "cols"), P("rows", "cols")),
        check_vma=False,
    )
```

time: 688 us -> 240 us (0.35)
  waiting for transfers between devices: 576 us -> 86.8 us
  starting transfers between devices: 0.35 us -> 36.6 us
    psum x3 -> x0, waiting for transfers between devices: 363 us -> none  [the longest x2 238 us: shards(): lax.psum((inner_rows(panel_block, panel_block), inner_rows(panel_block, t...]
    reduce_scatter x1 -> x0, waiting for transfers between devices: 213 us -> none  [shards(): lax.psum_scatter(product(gaussian, matrix), 'rows', scatter_dimension=0,...]
    all_to_all x0 -> x4, waiting for transfers between devices: none -> 46.2 us  [the longest x2 19.1 us: scatter_sum(): return jnp.sum(lax.all_to_all(pieces, axis, 0, 0, tiled=True), axis=0)]
    all_gather x0 -> x1, waiting for transfers between devices: none -> 40.6 us  [shards(): panel_block = lax.all_gather(part, 'cols', tiled=True)]
    all_to_all x0 -> x4, starting transfers between devices: none -> 36.5 us  [the longest x2 18.4 us: scatter_sum(): return jnp.sum(lax.all_to_all(pieces, axis, 0, 0, tiled=True), axis=0)]
  transfers between devices with their start and end apart: 4 -> 5, of which waited for: 4 -> 5; matrix products, arithmetic and copies ran while one was open for 12% -> 4% of each run, Pallas kernels for 0% -> 0%
where the time goes in v1:
time: 240 us; the launch traced here: 236 us
  waiting for transfers between devices  86.8 us (36%)
  other arithmetic  56.4 us (24%)
  starting transfers between devices  36.6 us (15%)
  matrix products  28.9 us (12%)
  between operations  15.7 us (7%)
  local copies, waits for them, and re-layouts  11.6 us (5%)
    all_gather x1, waiting for transfers between devices, shards(): panel_block = lax.all_gather(part, 'cols', tiled=True)  40.6 us
    another operation x6, other arithmetic, factor_parts(): chol_factor = jnp.linalg.cholesky(gram_matrix)  34 us
    another operation x4, other arithmetic, factor_parts(): lax.linalg.triangular_solve(chol_factor, cross_terms, left_side=True, low...  21.2 us
    all_to_all x2, waiting for transfers between devices, scatter_sum(): return jnp.sum(lax.all_to_all(pieces, axis, 0, 0, tiled=True), axis=0)  19.1 us
    dot_general x6, matrix products, product(): jnp.dot(left, right, precision=lax.Precision.HIGHEST, preferred_element_t...  18.6 us
    all_to_all x2, starting transfers between devices, scatter_sum(): return jnp.sum(lax.all_to_all(pieces, axis, 0, 0, tiled=True), axis=0)  18.4 us
    all_to_all x1, waiting for transfers between devices, shards(): lax.all_to_all(mine.reshape(col_groups, rows_dev // col_groups, MOST), 'c...  17.3 us
    all_to_all x1, starting transfers between devices, shards(): lax.all_to_all(mine.reshape(col_groups, rows_dev // col_groups, MOST), 'c...  10.2 us
  transfers between devices with their start and end apart: 5, of which 5 were waited for; matrix products, arithmetic and copies ran while one was open for 4% of the time, Pallas kernels for 0%

profile of v1, /device:TPU:1, one launch (start us, length us, event | category | flops | bytes accessed | tf_op | source)
XLA Modules:
  0.0 236.1 jit_solution(10165952061545958769)
XLA Ops:
  7.2 0.8 and_select_fusion
  8.0 0.2 convert_reduce_fusion
  8.2 0.3 fusion.4
  8.5 0.3 copy-done
  8.8 2.1 convolution_bitcast_fusion
  10.9 0.8 copy.25
  11.7 10.2 %all-to-all-start.1 = ((f32[16,128,64]{1,2,0:T(8,128)}), f32[16,128,64]{1,2,0:T(8,128)S(1)}, u32[]{:S(2)}, u32[]{:S(2)}) async-start(f32[16,128,64]{1,2,0:T(8,128)} %bitcast.56), calls=%async_computation.1 | async-start | bytes 1048576 | tf_op jit(solution)/shard_map/all_to_all | solution.py:62
  22.1 17.3 %all-to-all-done.1 = f32[16,128,64]{1,2,0:T(8,128)S(1)} async-done(((f32[16,128,64]{1,2,0:T(8,128)}), f32[16,128,64]{1,2,0:T(8,128)S(1)}, u32[]{:S(2)}, u32[]{:S(2)}) %all-to-all-start.1) | async-done | bytes 524320 | tf_op jit(solution)/shard_map/all_to_all | solution.py:62
  39.3 1.4 convolution_bitcast_fusion.2
  40.8 40.6 %all-gather.2.cloned.1.call-done = f32[2048,256]{1,0:T(8,128)} async-done(((f32[128,256]{1,0:T(8,128)}), f32[2048,256]{1,0:T(8,128)}) %all-gather.2.cloned.1.call-update) | async-done | bytes 2097168 | tf_op jit(solution)/shard_map/all_gather | solution.py:76
  81.4 5.8 %fusion.24 = f32[256,256]{0,1:T(8,128)S(1)} fusion(f32[2048,256]{1,0:T(8,128)} %all-gather.2.cloned.1.call-done), kind=kOutput, calls=%fused_computation.66 | convolution fusion | flops 1610612736 | bytes 2359296 | tf_op jit(solution)/shard_map/dot_general | solution.py:10
  87.2 3.6 %convolution_bitcast_fusion.1 = f32[256,256]{0,1:T(8,128)S(1)} fusion(f32[2048,256]{1,0:T(8,128)S(1)} %copy-done.1, f32[256,2048]{1,0:T(8,128)S(1)} %copy-done.2), kind=kOutput, calls=%fused_computation.4 | convolution fusion | flops 1610612736 | bytes 4456448 | tf_op jit(solution)/shard_map/dot_general | solution.py:20
  90.9 1.2 fusion.25
  92.1 1.1 copy.17
  93.2 10.1 %all-to-all-start.2 = ((f32[32,8,544]{2,1,0:T(8,128)}), f32[32,8,544]{2,1,0:T(8,128)S(1)}, u32[]{:S(2)}, u32[]{:S(2)}) async-start(f32[32,8,544]{2,1,0:T(8,128)} %bitcast.4), calls=%async_computation.2 | async-start | bytes 1310720 | tf_op jit(solution)/shard_map/all_to_all | solution.py:35
  103.3 3.6 %fusion.23 = f32[256,32]{0,1:T(8,128)S(1)} fusion(f32[256,2048]{1,0:T(8,128)} %param.5, f32[2048,32]{0,1:T(8,128)S(1)} %copy-done.4), kind=kOutput, calls=%fused_computation.65 | convolution fusion | flops 201326592 | bytes 2392064 | tf_op jit(solution)/shard_map/dot_general | solution.py:20
  106.9 3.5 %fusion.22 = f32[256,256]{0,1:T(8,128)S(1)} fusion(f32[256,2048]{1,0:T(8,128)S(1)} %copy-done.3, f32[2048,256]{1,0:T(8,128)S(1)} %copy-done), kind=kOutput, calls=%fused_computation.64 | convolution fusion | flops 1610612736 | bytes 4456448 | tf_op jit(solution)/shard_map/dot_general | solution.py:20
  110.4 0.9 copy.15
  111.4 8.4 %all-to-all-done.2 = f32[32,8,544]{2,1,0:T(8,128)S(1)} async-done(((f32[32,8,544]{2,1,0:T(8,128)}), f32[32,8,544]{2,1,0:T(8,128)S(1)}, u32[]{:S(2)}, u32[]{:S(2)}) %all-to-all-start.2) | async-done | bytes 557088 | tf_op jit(solution)/shard_map/all_to_all | solution.py:35
  119.7 8.3 %all-to-all-start = ((f32[32,8,288]{2,1,0:T(8,128)}), f32[32,8,288]{2,1,0:T(8,128)S(1)}, u32[]{:S(2)}, u32[]{:S(2)}) async-start(f32[32,8,288]{2,1,0:T(8,128)} %bitcast.67), calls=%async_computation | async-start | bytes 786432 | tf_op jit(solution)/shard_map/all_to_all | solution.py:35
  128.2 10.7 %all-to-all-done = f32[32,8,288]{2,1,0:T(8,128)S(1)} async-done(((f32[32,8,288]{2,1,0:T(8,128)}), f32[32,8,288]{2,1,0:T(8,128)S(1)}, u32[]{:S(2)}, u32[]{:S(2)}) %all-to-all-start) | async-done | bytes 294944 | tf_op jit(solution)/shard_map/all_to_all | solution.py:35
  138.9 0.8 broadcast_in_dim.3
  139.7 7.9 %all-to-all-start.3 = ((f32[32,8,288]{2,1,0:T(8,128)}), f32[32,8,288]{2,1,0:T(8,128)S(1)}, u32[]{:S(2)}, u32[]{:S(2)}) async-start(f32[32,8,288]{2,1,0:T(8,128)} %broadcast_in_dim.3), calls=%async_computation.3 | async-start | bytes 786432 | tf_op jit(solution)/shard_map/all_to_all | solution.py:41
  147.7 0.6 slice.90
  148.3 9.8 %all-to-all-done.3 = f32[32,8,288]{2,1,0:T(8,128)S(1)} async-done(((f32[32,8,288]{2,1,0:T(8,128)}), f32[32,8,288]{2,1,0:T(8,128)S(1)}, u32[]{:S(2)}, u32[]{:S(2)}) %all-to-all-start.3) | async-done | bytes 294944 | tf_op jit(solution)/shard_map/all_to_all | solution.py:41
  158.3 11.7 %cholesky.50 = f32[128,128]{1,0:T(8,128)S(1)} custom-call(f32[128,128]{1,0:T(8,128)S(1)} %cholesky.118), custom_call_target="Cholesky" | custom-call | tf_op jit(solution)/shard_map/jit(cholesky)/cholesky | solution.py:24
  170.1 0.6 triangular_solve.90
  170.7 9.8 %custom-call.16 = f32[1,128,128]{1,2,0:T(8,128)S(1)} custom-call(f32[1,128,128]{2,1,0:T(8,128)S(1)} %get-tuple-element.25), custom_call_target="InvertDiagBlocksLowerTriangular" | custom-call | tf_op jit(solution)/shard_map/jit(cholesky)/cholesky | solution.py:24
  180.5 0.2 constant_dynamic-update-slice_fusion.1
  180.7 0.3 convolution_subtract_fusion.1
  181.0 11.7 %cholesky.105 = f32[128,128]{1,0:T(8,128)S(1)} custom-call(f32[128,128]{1,0:T(8,128)S(1)} %convolution_subtract_fusion.1), custom_call_target="Cholesky" | custom-call | tf_op jit(solution)/shard_map/jit(cholesky)/cholesky | solution.py:24
  192.8 0.7 compare_reduce_fusion
  194.9 5.3 %while.1 = (s32[]{:T(128)}, f32[256,256]{1,0:T(8,128)S(1)}, s32[2,2]{1,0:T(2,128)S(1)}, f32[2,128,128]{2,1,0:T(8,128)}, s32[]{:T(128)}) while((s32[]{:T(128)}, f32[256,256]{1,0:T(8,128)S(1)}, s32[2,2]{1,0:T(2,128)S(1)}, f32[2,128,128]{2,1,0:T(8,128)}, s32[]{:T(128)}) %tuple.28), condition=%wide.while_cond, body=%wide.while_body.sunk | while | flops 2 | bytes 132705 | solution.py:25
  194.9 0.6 fusion.48
  195.5 2.0 bitcast_dynamic-update-slice_fusion.2
  197.6 0.6 fusion.48
  198.1 2.0 bitcast_dynamic-update-slice_fusion.2
  200.2 20.5 %custom-call.17 = f32[2,128,128]{1,2,0:T(8,128)S(1)} custom-call(f32[2,128,128]{2,1,0:T(8,128)} %get-tuple-element.11), custom_call_target="InvertDiagBlocksLowerTriangular" | custom-call | tf_op jit(solution)/shard_map/triangular_solve | solution.py:25
  220.7 0.3 fusion.7
  221.0 0.9 copy.22
  221.8 0.2 convolution_subtract_fusion.3
  222.1 0.2 fusion.15
  222.3 0.2 fusion.14
  222.5 0.6 pad_maximum_fusion.2
  223.1 0.2 convolution_subtract_fusion.2
  223.3 0.2 fusion.13
  223.5 1.5 convolution_subtract_fusion.4
  225.0 4.3 %convolution_subtract_fusion = f32[2048,32]{0,1:T(8,128)} fusion(f32[2048,32]{0,1:T(8,128)S(1)} %copy-done.4, f32[2048,256]{1,0:T(8,128)} %all-gather.2.cloned.1.call-done, f32[128,32]{0,1:T(8,128)S(1)} %fusion.14, f32[128,32]{0,1:T(8,128)S(1)} %fusion.13), kind=kOutput, calls=%fused_computation.2 | convolution fusion | flops 201400320 | bytes 2654208 | tf_op jit(solution)/shard_map/dot_general | solution.py:20
  (35 shorter events, 0.7 us)
Async XLA Ops:
  7.2 1.6 copy-start
  11.7 27.6 %all-to-all-start.1 = ((f32[16,128,64]{1,2,0:T(8,128)}), f32[16,128,64]{1,2,0:T(8,128)S(1)}, u32[]{:S(2)}, u32[]{:S(2)}) async-start(f32[16,128,64]{1,2,0:T(8,128)} %bitcast.56), calls=%async_computation.1 | async-start | bytes 1048576 | tf_op jit(solution)/shard_map/all_to_all | solution.py:62
  22.0 59.4 %all-gather.2.cloned.1.call-start = ((), (), s32[]{:S(2)}) async-start(), calls=%async_computation.4 | async-start | bytes 2228224 | tf_op jit(solution)/shard_map/all_gather | solution.py:76
  81.4 5.8 %copy-start.1 = (f32[2048,256]{1,0:T(8,128)S(1)}, f32[2048,256]{1,0:T(8,128)}, u32[]{:S(2)}) copy-start(f32[2048,256]{1,0:T(8,128)} %all-gather.2.cloned.1.call-done) | copy-start | bytes 6291460
  81.4 5.8 %copy-start.2 = (f32[256,2048]{1,0:T(8,128)S(1)}, f32[256,2048]{1,0:T(8,128)}, u32[]{:S(2)}) copy-start(f32[256,2048]{1,0:T(8,128)} %param.5) | copy-start | bytes 6291460
  87.2 3.6 %copy-start.4 = (f32[2048,32]{0,1:T(8,128)S(1)}, f32[2048,32]{0,1:T(8,128)}, u32[]{:S(2)}) copy-start(f32[2048,32]{0,1:T(8,128)} %param.7) | copy-start | bytes 786436
  93.2 26.6 %all-to-all-start.2 = ((f32[32,8,544]{2,1,0:T(8,128)}), f32[32,8,544]{2,1,0:T(8,128)S(1)}, u32[]{:S(2)}, u32[]{:S(2)}) async-start(f32[32,8,544]{2,1,0:T(8,128)} %bitcast.4), calls=%async_computation.2 | async-start | bytes 1310720 | tf_op jit(solution)/shard_map/all_to_all | solution.py:35
  103.3 3.6 %copy-start.3 = (f32[256,2048]{1,0:T(8,128)S(1)}, f32[256,2048]{1,0:T(8,128)}, u32[]{:S(2)}) copy-start(f32[256,2048]{1,0:T(8,128)} %param.5) | copy-start | bytes 6291460
  119.7 19.2 %all-to-all-start = ((f32[32,8,288]{2,1,0:T(8,128)}), f32[32,8,288]{2,1,0:T(8,128)S(1)}, u32[]{:S(2)}, u32[]{:S(2)}) async-start(f32[32,8,288]{2,1,0:T(8,128)} %bitcast.67), calls=%async_computation | async-start | bytes 786432 | tf_op jit(solution)/shard_map/all_to_all | solution.py:35
  128.2 30.0 %copy-start.5 = (f32[8,544]{1,0:T(8,128)}, f32[8,544]{1,0:T(8,128)S(1)}, u32[]{:S(2)}) copy-start(f32[8,544]{1,0:T(8,128)S(1)} %reduce_sum.29) | copy-start | bytes 52228
  139.7 18.4 %all-to-all-start.3 = ((f32[32,8,288]{2,1,0:T(8,128)}), f32[32,8,288]{2,1,0:T(8,128)S(1)}, u32[]{:S(2)}, u32[]{:S(2)}) async-start(f32[32,8,288]{2,1,0:T(8,128)} %broadcast_in_dim.3), calls=%async_computation.3 | async-start | bytes 786432 | tf_op jit(solution)/shard_map/all_to_all | solution.py:41
Sparse Core Ops, SparseCore 0:
  40.9 40.4 all-gather.1

commit v2 on v0

v2 whole, which is shorter than its diff:
```python
import functools
import jax
import jax.numpy as jnp
from jax import lax
from jax.experimental import pallas as pl
from jax.experimental.pallas import tpu as pltpu
from jax.sharding import PartitionSpec as P

MOST = 64
BLOCK = 64
STEP = 8
LANES = 128
VMEM = pl.BlockSpec(memory_space=pltpu.VMEM)
PARAMS = pltpu.CompilerParams(vmem_limit_bytes=48 * 1024 * 1024)


def product(left, right):
    return jnp.dot(left, right, precision=lax.Precision.HIGHEST, preferred_element_type=jnp.float32)


def dot(left, right, left_dim, right_dim):
    return lax.dot_general(
        left,
        right,
        (((left_dim,), (right_dim,)), ((), ())),
        precision=lax.Precision.HIGHEST,
        preferred_element_type=jnp.float32,
    )


def hot_dot(hot, values, hot_dim, value_dim):
    high = values.astype(jnp.bfloat16)
    rest = values - high.astype(jnp.float32)
    middle = rest.astype(jnp.bfloat16)
    low = (rest - middle.astype(jnp.float32)).astype(jnp.bfloat16)
    dims = (((hot_dim,), (value_dim,)), ((), ()))
    parts = [
        lax.dot_general(hot, piece, dims, preferred_element_type=jnp.float32)
        for piece in (high, middle, low)
    ]
    return parts[0] + parts[1] + parts[2]


def dot_hot(values, hot):
    high = values.astype(jnp.bfloat16)
    rest = values - high.astype(jnp.float32)
    middle = rest.astype(jnp.bfloat16)
    low = (rest - middle.astype(jnp.float32)).astype(jnp.bfloat16)
    parts = [
        jnp.dot(piece, hot, preferred_element_type=jnp.float32) for piece in (high, middle, low)
    ]
    return parts[0] + parts[1] + parts[2]


def cost(micros):
    return pl.CostEstimate(flops=int(micros * 1e9), bytes_accessed=0, transcendentals=0)


def iota(shape, dim):
    return lax.broadcasted_iota(jnp.int32, shape, dim)


def pick_kernel(block_ref, column_ref, row_ref, matrix_ref, out_ref, pick_ref):
    width = matrix_ref.shape[1]
    count = row_ref.shape[1]

    @pl.when(pl.program_id(0) == 0)
    def _():
        row = row_ref[...]
        owner_row = row // width
        same = (column_ref[...] // width == owner_row) & (
            iota((count, count), 0) < iota((count, count), 1)
        )
        slot_row = jnp.sum(same.astype(jnp.int32), axis=0, keepdims=True)
        local_row = row - block_ref[0] * width
        by_slot = (iota((MOST, count), 0) == slot_row).astype(jnp.bfloat16)
        by_column = (iota((width, count), 0) == local_row).astype(jnp.bfloat16)
        pick_ref[...] = lax.dot_general(
            by_slot, by_column, (((1,), (1,)), ((), ())), preferred_element_type=jnp.float32
        ).astype(jnp.bfloat16)

    got = hot_dot(pick_ref[...], matrix_ref[...], 1, 1)
    for piece in range(out_ref.shape[0]):
        out_ref[piece] = got[:, piece * LANES : (piece + 1) * LANES]


def pick_columns(block, pivots, matrix, steps=4):
    rows_dev, cols_dev = matrix.shape
    count = pivots.shape[0]
    pieces = rows_dev // LANES
    return pl.pallas_call(
        pick_kernel,
        grid=(steps,),
        out_shape=jax.ShapeDtypeStruct((pieces, MOST, LANES), jnp.float32),
        in_specs=[
            pl.BlockSpec(memory_space=pltpu.SMEM),
            pl.BlockSpec((count, 1), lambda i: (0, 0)),
            pl.BlockSpec((1, count), lambda i: (0, 0)),
            pl.BlockSpec((rows_dev // steps, cols_dev), lambda i: (i, 0)),
        ],
        out_specs=pl.BlockSpec((pieces // steps, MOST, LANES), lambda i: (i, 0, 0)),
        scratch_shapes=[pltpu.VMEM((MOST, cols_dev), jnp.bfloat16)],
        compiler_params=PARAMS,
        cost_estimate=cost(2),
        name="pick_columns",
    )(block, pivots.reshape(count, 1), pivots.reshape(1, count), matrix)


def sketch_kernel(gaussian_ref, matrix_ref, slab_ref, out_ref):
    width = matrix_ref.shape[1]
    gaussian = gaussian_ref[...]
    out_ref[:, :width] = dot(gaussian, matrix_ref[...], 1, 0)
    out_ref[:, width:] = dot(gaussian, slab_ref[...], 1, 1)


def sketch_sums(gaussian, matrix, slab):
    return pl.pallas_call(
        sketch_kernel,
        out_shape=jax.ShapeDtypeStruct(
            (gaussian.shape[0], matrix.shape[1] + slab.shape[0]), jnp.float32
        ),
        in_specs=[VMEM] * 3,
        out_specs=VMEM,
        compiler_params=PARAMS,
        cost_estimate=cost(4),
        name="sketch_sums",
    )(gaussian, matrix, slab)


def part_kernel(width, column_ref, row_ref, spread_ref, sketch_ref, part_ref, send_ref):
    count = row_ref.shape[1]
    slots = spread_ref.shape[0]
    column = column_ref[...]
    owner = column // width
    same = (owner == row_ref[...] // width) & (iota((count, count), 1) < iota((count, count), 0))
    slot = jnp.sum(same.astype(jnp.int32), axis=1, keepdims=True)
    place = (iota((count, slots), 1) == owner * MOST + slot).astype(jnp.bfloat16)
    part = hot_dot(place, spread_ref[...], 1, 0)
    part_ref[...] = part
    send_ref[:, :, :count] = dot(part, part, 1, 1).reshape(send_ref.shape[0], -1, count)
    send_ref[:, :, count:] = sketch_ref[...]


def part_products(width, pivots, spread, sketch):
    count = pivots.shape[0]
    pieces, rows, lanes = sketch.shape
    return pl.pallas_call(
        functools.partial(part_kernel, width),
        out_shape=(
            jax.ShapeDtypeStruct((count, LANES), jnp.float32),
            jax.ShapeDtypeStruct((pieces, rows, count + lanes), jnp.float32),
        ),
        in_specs=[VMEM] * 4,
        out_specs=(VMEM,) * 2,
        compiler_params=PARAMS,
        cost_estimate=cost(2),
        name="part_products",
    )(pivots.reshape(count, 1), pivots.reshape(1, count), spread, sketch)


def row_sums_kernel(block_ref, row_ref, got_ref, send_ref, sketch_ref, trail_ref):
    width = sketch_ref.shape[1]
    count = row_ref.shape[1]
    total = jnp.sum(got_ref[...], axis=0)
    sketch = total[:, count : count + width]
    sketch_ref[...] = sketch
    trail_ref[...] = total[:, count + width :]
    local_row = row_ref[...] - block_ref[0] * width
    by_column = (iota((width, count), 0) == local_row).astype(jnp.bfloat16)
    both = jnp.concatenate([total[:, :count], dot_hot(sketch, by_column)], axis=1)
    for piece in range(send_ref.shape[0]):
        send_ref[piece] = both


def row_sums(block, pivots, got, width, pieces):
    count = pivots.shape[0]
    _, rows, lanes = got.shape
    return pl.pallas_call(
        row_sums_kernel,
        out_shape=(
            jax.ShapeDtypeStruct((pieces, rows, 2 * count), jnp.float32),
            jax.ShapeDtypeStruct((rows, width), jnp.float32),
            jax.ShapeDtypeStruct((rows, lanes - count - width), jnp.float32),
        ),
        in_specs=[pl.BlockSpec(memory_space=pltpu.SMEM), VMEM, VMEM],
        out_specs=(VMEM,) * 3,
        compiler_params=PARAMS,
        cost_estimate=cost(1),
        name="row_sums",
    )(block, pivots.reshape(1, count), got)


def col_sums_kernel(got_ref, panel_ref, slab_ref, send_ref, gauss_ref):
    total = jnp.sum(got_ref[...], axis=0)
    count = gauss_ref.shape[1]
    gauss_ref[...] = total[:, count:]
    rows = total.shape[0]
    cross = jnp.zeros((count, slab_ref.shape[0]), jnp.float32)
    for piece in range(panel_ref.shape[0]):
        at = slice(piece * LANES, (piece + 1) * LANES)
        cross += dot(panel_ref[piece], slab_ref[:, at], 1, 1)
    for piece in range(send_ref.shape[0]):
        send_ref[piece, :, :count] = total[:, :count]
        send_ref[piece, :, count:] = cross[piece * rows : (piece + 1) * rows]


def col_sums(got, panel, slab, pieces):
    _, rows, both = got.shape
    count = both // 2
    return pl.pallas_call(
        col_sums_kernel,
        out_shape=(
            jax.ShapeDtypeStruct((pieces, rows, count + slab.shape[0]), jnp.float32),
            jax.ShapeDtypeStruct((rows, count), jnp.float32),
        ),
        in_specs=[VMEM] * 3,
        out_specs=(VMEM,) * 2,
        compiler_params=PARAMS,
        cost_estimate=cost(2),
        name="col_sums",
    )(got, panel, slab)


def cross_sums_kernel(got_ref, send_ref):
    count = got_ref.shape[2] - send_ref.shape[2]
    total = jnp.sum(got_ref[:, :, count:], axis=0)
    for piece in range(send_ref.shape[0]):
        send_ref[piece] = total


def cross_sums(got, slab_cols):
    pieces, rows, _ = got.shape
    return pl.pallas_call(
        cross_sums_kernel,
        out_shape=jax.ShapeDtypeStruct((pieces, rows, slab_cols), jnp.float32),
        in_specs=[VMEM],
        out_specs=VMEM,
        compiler_params=PARAMS,
        cost_estimate=cost(1),
        name="cross_sums",
    )(got)


def block_inverse(block):
    n = block.shape[0]
    groups = n // 8
    sub = iota((8, 2 * n), 0)
    eye = (iota((n, n), 0) == iota((n, n), 1)).astype(jnp.float32)
    whole = jnp.concatenate([block, eye], axis=1)
    rows = [whole[8 * g : 8 * g + 8] for g in range(groups)]
    diag = [jnp.ones((8, 2 * n), jnp.float32) for _ in rows]
    for first in range(0, n, STEP):
        cols = [
            {
                g: jnp.broadcast_to(rows[g][:, j : j + 1], (8, 2 * n))
                for g in range(first // 8, groups)
            }
            for j in range(first, first + STEP)
        ]
        for t in range(STEP):
            k = first + t
            at, s = k // 8, k % 8
            col = cols[t]
            pivot = jnp.broadcast_to(col[at][s : s + 1], (8, 2 * n))
            inverse = 1.0 / pivot
            diag[at] = jnp.where(sub == s, pivot, diag[at])
            scaled = jnp.broadcast_to(rows[at][s : s + 1], (8, 2 * n)) * inverse
            for u in range(t + 1, STEP):
                other = jnp.broadcast_to(cols[u][at][s : s + 1], (8, 2 * n)) * inverse
                for g in range(at, groups):
                    cols[u][g] = cols[u][g] - col[g] * other
            for g in range(at, groups):
                factor = col[g] if g > at else jnp.where(sub > s, col[g], 0.0)
                rows[g] = rows[g] - factor * scaled
    out = jnp.concatenate([r * lax.rsqrt(d) for r, d in zip(rows, diag)], axis=0)
    return out[:, n:]


def inverse_kernel(gram_ref, out_ref, work):
    n = out_ref.shape[0]
    work[:, :n] = gram_ref[:, :, :n].reshape(n, n)
    work[:, n:] = (iota((n, n), 0) == iota((n, n), 1)).astype(jnp.float32)
    for top in range(0, n, BLOCK):
        end = top + BLOCK
        inv = block_inverse(work[top:end, top:end])
        if end == n:
            out_ref[top:end, :] = dot(inv, work[top:end, n:], 1, 0)
            break
        lo = end // LANES * LANES
        hi = -(-(n + end) // LANES) * LANES
        strip = dot(inv, work[top:end, lo:hi], 1, 0)
        done = strip[:, n - lo :]
        if hi < 2 * n:
            done = jnp.concatenate([done, jnp.zeros((BLOCK, 2 * n - hi), jnp.float32)], axis=1)
        out_ref[top:end, :] = done
        work[end:, lo:hi] -= dot(strip[:, end - lo : n - lo], strip, 0, 0)


def inverse_factor(gram):
    n = gram.shape[0] * gram.shape[1]
    return pl.pallas_call(
        inverse_kernel,
        out_shape=jax.ShapeDtypeStruct((n, n), jnp.float32),
        in_specs=[VMEM],
        out_specs=VMEM,
        scratch_shapes=[pltpu.VMEM((n, 2 * n), jnp.float32)],
        compiler_params=PARAMS,
        cost_estimate=cost(10),
        name="inverse_factor",
    )(gram)


def finish_kernel(inv_ref, cross_ref, panel_ref, slab_ref, gauss_ref, trail_ref, coupling_ref, projected_ref, sketch_ref):
    inv = inv_ref[...]
    coupling = dot(cross_ref[...], inv, 0, 1)
    coupling_ref[...] = coupling
    weights = dot(coupling, inv, 1, 0)
    for piece in range(panel_ref.shape[0]):
        at = slice(piece * LANES, (piece + 1) * LANES)
        projected_ref[:, at] = slab_ref[:, at] - dot(weights, panel_ref[piece], 1, 0)
    sketch_ref[...] = trail_ref[...] - dot(gauss_ref[...], weights, 1, 1)


def finish(inv, cross, panel, slab, gauss_panel, gauss_trail):
    return pl.pallas_call(
        finish_kernel,
        out_shape=(
            jax.ShapeDtypeStruct(cross.shape[::-1], jnp.float32),
            jax.ShapeDtypeStruct(slab.shape, jnp.float32),
            jax.ShapeDtypeStruct(gauss_trail.shape, jnp.float32),
        ),
        in_specs=[VMEM] * 6,
        out_specs=(VMEM,) * 3,
        compiler_params=PARAMS,
        cost_estimate=cost(3),
        name="finish",
    )(inv, cross, panel, slab, gauss_panel, gauss_trail)


def exchange(pieces, axis):
    return lax.all_to_all(pieces, axis, 0, 0, tiled=True)


def shards(matrix, gaussian, pivots, trailing):
    rows_dev, cols_dev = matrix.shape
    count = pivots.shape[0]
    slab_cols = trailing.shape[1]
    n_rows = lax.axis_size("rows")
    n_cols = lax.axis_size("cols")
    block = lax.axis_index("cols").reshape(1)
    slab = trailing.T

    mine = pick_columns(block, pivots, matrix)
    spread = exchange(mine, "cols")
    late_gaussian, mine = lax.optimization_barrier((gaussian, mine))
    sketch_part = sketch_sums(late_gaussian, matrix, slab)

    part, send = part_products(
        cols_dev,
        pivots,
        spread.reshape(n_cols * MOST, LANES),
        sketch_part.reshape(n_rows, -1, cols_dev + slab_cols),
    )
    panel = lax.all_gather(part, "cols")
    send, sketch, gauss_trail = row_sums(block, pivots, exchange(send, "rows"), cols_dev, n_cols)
    send, gauss_panel = col_sums(exchange(send, "cols"), panel, slab, n_rows)
    got = exchange(send, "rows")
    cross = exchange(cross_sums(got, slab_cols), "rows").reshape(count, slab_cols)
    inv = inverse_factor(got)
    coupling, projected, trailing_sketch = finish(
        inv, cross, panel, slab, gauss_panel, gauss_trail
    )
    return (sketch, coupling.T, projected.T, trailing_sketch)


def solution(mesh):
    placed = (P("rows", "cols"), P(None, "rows"), P(), P("rows", "cols"))
    return jax.shard_map(
        shards,
        mesh=mesh,
        in_specs=placed,
        out_specs=(P("rows", "cols"), P(None, "cols"), P("rows", "cols"), P("rows", "cols")),
        check_vma=False,
    )
```

time: 688 us -> 141 us (0.20)
  waiting for transfers between devices: 576 us -> 11.5 us
  blocking collectives: 0 us -> 63.8 us
  other arithmetic: 57.5 us -> 0.72 us
  matrix products: 28.2 us -> 0 us
  Pallas kernels: 0 us -> 22.9 us
  starting transfers between devices: 0.35 us -> 18.1 us
    psum x3 -> x0, waiting for transfers between devices: 363 us -> none  [the longest x2 238 us: shards(): lax.psum((inner_rows(panel_block, panel_block), inner_rows(panel_block, t...]
    reduce_scatter x1 -> x0, waiting for transfers between devices: 213 us -> none  [shards(): lax.psum_scatter(product(gaussian, matrix), 'rows', scatter_dimension=0,...]
    all_to_all x0 -> x3, blocking collectives: none -> 63.8 us  [exchange(): return lax.all_to_all(pieces, axis, 0, 0, tiled=True)]
    another operation x10 -> x0, other arithmetic: 54.4 us -> none  [the longest x6 34.1 us: factor_parts(): chol_factor = jnp.linalg.cholesky(gram_matrix)]
    dot_general x8 -> x0, matrix products: 25.2 us -> none  [the longest x6 17.7 us: product(): jnp.dot(left, right, precision=lax.Precision.HIGHEST, preferred_element_t...]
    pallas_call x0 -> x8, Pallas kernels: none -> 22.9 us  [the longest x1 9.86 us: inverse_factor(): pl.pallas_call(inverse_kernel, out_shape=jax.ShapeDtypeStruct((n, n), jnp...]
    all_to_all x0 -> x2, starting transfers between devices: none -> 18 us  [exchange(): return lax.all_to_all(pieces, axis, 0, 0, tiled=True)]
    all_to_all x0 -> x2, waiting for transfers between devices: none -> 11.5 us  [exchange(): return lax.all_to_all(pieces, axis, 0, 0, tiled=True)]
  transfers between devices with their start and end apart: 4 -> 3, of which waited for: 4 -> 1; matrix products, arithmetic and copies ran while one was open for 12% -> 0% of each run, Pallas kernels for 0% -> 10%
where the time goes in v2:
time: 141 us; the launch traced here: 140 us
  blocking collectives  63.8 us (45%)
  Pallas kernels  22.9 us (16%)
  starting transfers between devices  18.1 us (13%)
  between operations  14.2 us (10%)
  waiting for transfers between devices  11.5 us (8%)
  local copies, waits for them, and re-layouts  9.33 us (7%)
    all_to_all x3, blocking collectives, exchange(): return lax.all_to_all(pieces, axis, 0, 0, tiled=True)  63.8 us
    all_to_all x2, starting transfers between devices, exchange(): return lax.all_to_all(pieces, axis, 0, 0, tiled=True)  18 us
    all_to_all x2, waiting for transfers between devices, exchange(): return lax.all_to_all(pieces, axis, 0, 0, tiled=True)  11.5 us
    pallas_call x1, Pallas kernels, inverse_factor(): pl.pallas_call(inverse_kernel, out_shape=jax.ShapeDtypeStruct((n, n), jnp...  9.86 us
    unnamed x24, local copies, waits for them, and re-layouts  8.01 us
    pallas_call x1, Pallas kernels, sketch_sums(): pl.pallas_call(sketch_kernel, out_shape=jax.ShapeDtypeStruct((gaussian.sh...  3.43 us
  transfers between devices with their start and end apart: 3, of which 1 were waited for; matrix products, arithmetic and copies ran while one was open for 0% of the time, Pallas kernels for 10%

profile of v2, /device:TPU:1, one launch (start us, length us, event | category | flops | bytes accessed | tf_op | source)
XLA Modules:
  0.0 140.5 jit_solution(13460120299419021785)
XLA Ops:
  7.2 0.8 copy.9.column_ref
  8.0 0.0 copy-start
  8.0 0.7 copy-done
  8.7 0.0 copy-start.2
  8.7 1.6 %copy-done.2 = f32[2048,256]{1,0:T(8,128)S(1)} copy-done((f32[2048,256]{1,0:T(8,128)S(1)}, f32[2048,256]{1,0:T(8,128)}, u32[]{:S(2)}) %copy-start.2) | copy-done | bytes 2097176
  10.3 0.0 copy-start.3
  10.3 0.0 copy-start.7
  10.3 2.7 %pick_columns.1 = f32[16,64,128]{2,1,0:T(8,128)} custom-call(s32[1]{0:T(128)} %bitcast.block_ref, s32[256,1]{1,0:T(8,128)S(1)} %copy.9.column_ref, s32[1,256]{1,0:T(1,128)S(1)} %bitcast.13, f32[2048,256]{1,0:T(8,128)S(1)} %copy-done.2), custom_call_target="tpu_custom_call" | custom-call | flops 2000000000 | tf_op jit(solution)/shard_map/pick_columns/pallas_call | solution.py:91
  13.0 10.2 %all-to-all-start = ((f32[16,64,128]{2,1,0:T(8,128)}), f32[16,64,128]{2,1,0:T(8,128)S(1)}, u32[]{:S(2)}, u32[]{:S(2)}) async-start(f32[16,64,128]{2,1,0:T(8,128)} %pick_columns.1), calls=%async_computation | async-start | bytes 1048576 | tf_op jit(solution)/shard_map/all_to_all | solution.py:341
  23.2 0.0 all-gather.3.cloned.1.call-start
  23.2 0.0 copy-done.3
  23.2 0.0 copy-done.7
  23.3 0.0 copy-start.4
  23.3 1.6 %copy-done.4 = f32[256,2048]{1,0:T(8,128)S(1)} copy-done((f32[256,2048]{1,0:T(8,128)S(1)}, f32[256,2048]{1,0:T(8,128)}, u32[]{:S(2)}) %copy-start.4) | copy-done | bytes 2097176
  24.9 0.0 copy-start.1
  24.9 3.4 %sketch_sums.1 = f32[256,288]{1,0:T(8,128)S(1)} custom-call(f32[256,2048]{1,0:T(8,128)S(1)} %copy-done.4, f32[2048,256]{1,0:T(8,128)S(1)} %copy-done.3, f32[32,2048]{1,0:T(8,128)S(1)} %bitcast.18), custom_call_target="tpu_custom_call" | custom-call | flops 4000000000 | tf_op jit(solution)/shard_map/sketch_sums/pallas_call | solution.py:117
  28.3 0.0 copy-start.9
  28.3 0.7 copy-done.9
  29.0 11.5 %all-to-all-done = f32[16,64,128]{2,1,0:T(8,128)S(1)} async-done(((f32[16,64,128]{2,1,0:T(8,128)}), f32[16,64,128]{2,1,0:T(8,128)S(1)}, u32[]{:S(2)}, u32[]{:S(2)}) %all-to-all-start) | async-done | bytes 524320 | tf_op jit(solution)/shard_map/all_to_all | solution.py:341
  40.5 0.0 copy-done.1
  40.5 0.0 copy-start.10
  40.5 1.0 copy-done.10
  41.5 1.8 %part_products.1 = (f32[256,128]{1,0:T(8,128)}, f32[32,8,544]{2,1,0:T(8,128)S(1)}) custom-call(s32[256,1]{1,0:T(8,128)S(1)} %copy.9.column_ref, s32[1,256]{1,0:T(1,128)S(1)} %bitcast.14, f32[1024,128]{1,0:T(8,128)S(1)} %bitcast.10, f32[32,8,288]{2,1,0:T(8,128)S(1)} %bitcast.21), custom_call_target="tpu_custom_call" | custom-call | flops 2000000000 | tf_op jit(solution)/shard_map/part_products/pallas_call | solution.py:147
  43.3 0.0 all-gather.3.cloned.1.call-update
  43.4 30.3 %all_to_all.25.got_ref = f32[32,8,544]{2,1,0:T(8,128)S(1)} all-to-all(f32[32,8,544]{2,1,0:T(8,128)S(1)} %get-tuple-element.16), channel_id=1, replica_groups=mesh['rows'=32,'cols'=16] {'rows'}, dimensions={0} | all-to-all | bytes 1114112 | tf_op jit(solution)/shard_map/all_to_all | solution.py:341
  73.6 0.0 copy-start.8
  73.6 0.7 row_sums.1
  74.3 15.4 %all_to_all.26.got_ref = f32[16,8,512]{2,1,0:T(8,128)S(1)} all-to-all(f32[16,8,512]{2,1,0:T(8,128)S(1)} %get-tuple-element.18), channel_id=1, replica_groups=mesh['rows'=32,'cols'=16] {'cols'}, dimensions={0} | all-to-all | bytes 524288 | tf_op jit(solution)/shard_map/all_to_all | solution.py:341
  89.7 0.0 all-gather.3.cloned.1.call-done
  89.7 0.0 copy-done.8
  89.7 0.0 copy-start.5
  89.7 1.6 %copy-done.5 = f32[4096,128]{1,0:T(8,128)S(1)} copy-done((f32[4096,128]{1,0:T(8,128)S(1)}, f32[4096,128]{1,0:T(8,128)}, u32[]{:S(2)}) %copy-start.5) | copy-done | bytes 2097176
  91.3 1.8 %col_sums.1 = (f32[32,8,288]{2,1,0:T(8,128)S(1)}, f32[8,256]{1,0:T(8,128)S(1)}) custom-call(f32[16,8,512]{2,1,0:T(8,128)S(1)} %all_to_all.26.got_ref, f32[16,256,128]{2,1,0:T(8,128)S(1)} %bitcast.16, f32[32,2048]{1,0:T(8,128)S(1)} %bitcast.19), custom_call_target="tpu_custom_call" | custom-call | flops 2000000000 | tf_op jit(solution)/shard_map/col_sums/pallas_call | solution.py:210
  93.1 18.1 %all_to_all.27.gram_ref.got_ref = f32[32,8,288]{2,1,0:T(8,128)S(1)} all-to-all(f32[32,8,288]{2,1,0:T(8,128)S(1)} %get-tuple-element.20), channel_id=1, replica_groups=mesh['rows'=32,'cols'=16] {'rows'}, dimensions={0} | all-to-all | bytes 589824 | tf_op jit(solution)/shard_map/all_to_all | solution.py:341
  111.3 0.7 reshape.36
  112.0 7.8 %all-to-all-start.4 = ((f32[32,1,256]{2,1,0:T(1,128)}), f32[32,1,256]{2,1,0:T(1,128)S(1)}, u32[]{:S(2)}, u32[]{:S(2)}) async-start(f32[32,1,256]{2,1,0:T(1,128)} %reshape.36), calls=%async_computation.4 | async-start | bytes 65536 | tf_op jit(solution)/shard_map/all_to_all | solution.py:341
  119.8 0.0 copy-start.6
  119.8 9.9 %inverse_factor.1.inv_ref = f32[256,256]{1,0:T(8,128)S(1)} custom-call(f32[32,8,288]{2,1,0:T(8,128)S(1)} %all_to_all.27.gram_ref.got_ref), custom_call_target="tpu_custom_call" | custom-call | flops 10000000000 | tf_op jit(solution)/shard_map/inverse_factor/pallas_call | solution.py:301
  129.7 0.0 all-to-all-done.4
  129.7 0.5 broadcast
  130.2 0.7 reduce
  130.9 0.1 reshape.37
  131.0 0.0 copy-done.6
  131.0 2.6 %finish.1 = (f32[32,256]{1,0:T(8,128)}, f32[32,2048]{1,0:T(8,128)}, f32[8,32]{1,0:T(8,128)}) custom-call(f32[256,256]{1,0:T(8,128)S(1)} %inverse_factor.1.inv_ref, f32[256,32]{1,0:T(8,128)S(1)} %bitcast.11, f32[16,256,128]{2,1,0:T(8,128)S(1)} %bitcast.17, f32[32,2048]{1,0:T(8,128)S(1)} %bitcast.20, f32[8,256]{1,0:T(8,128)S(1)} %get-tuple-element.21.gauss_ref, ...), custom_call_target="tpu_custom_call" | custom-call | flops 3000000000 | tf_op jit(solution)/shard_map/finish/pallas_call | solution.py:325
  (1 shorter events, 0.0 us)
Async XLA Ops:
  8.0 0.7 copy-start
  8.7 1.6 %copy-start.2 = (f32[2048,256]{1,0:T(8,128)S(1)}, f32[2048,256]{1,0:T(8,128)}, u32[]{:S(2)}) copy-start(f32[2048,256]{1,0:T(8,128)} %matrix_ref.3) | copy-start | bytes 6291460
  10.3 13.0 %copy-start.3 = (f32[2048,256]{1,0:T(8,128)S(1)}, f32[2048,256]{1,0:T(8,128)}, u32[]{:S(2)}) copy-start(f32[2048,256]{1,0:T(8,128)} %matrix_ref.3) | copy-start | bytes 6291460
  10.3 13.0 %copy-start.7 = (f32[2048,32]{0,1:T(8,128)S(1)}, f32[2048,32]{0,1:T(8,128)}, u32[]{:S(2)}) copy-start(f32[2048,32]{0,1:T(8,128)} %param.7) | copy-start | bytes 786436
  13.0 27.6 %all-to-all-start = ((f32[16,64,128]{2,1,0:T(8,128)}), f32[16,64,128]{2,1,0:T(8,128)S(1)}, u32[]{:S(2)}, u32[]{:S(2)}) async-start(f32[16,64,128]{2,1,0:T(8,128)} %pick_columns.1), calls=%async_computation | async-start | bytes 1048576 | tf_op jit(solution)/shard_map/all_to_all | solution.py:341
  23.2 66.5 %all-gather.3.cloned.1.call-start = ((), (), s32[]{:S(2)}) async-start(), calls=%async_computation.5 | async-start | bytes 2228224 | tf_op jit(solution)/shard_map/all_gather | solution.py:364
  23.3 1.6 %copy-start.4 = (f32[256,2048]{1,0:T(8,128)S(1)}, f32[256,2048]{1,0:T(8,128)}, u32[]{:S(2)}) copy-start(f32[256,2048]{1,0:T(8,128)} %gaussian_ref) | copy-start | bytes 6291460
  24.9 15.7 %copy-start.1 = (s32[256]{0:T(256)S(1)}, s32[256]{0:T(256)}, u32[]{:S(2)}) copy-start(s32[256]{0:T(256)} %param.6) | copy-start | bytes 3076
  28.3 0.7 copy-start.9
  40.5 1.0 copy-start.10
  73.6 16.1 %copy-start.8 = (f32[2048,32]{0,1:T(8,128)S(1)}, f32[2048,32]{0,1:T(8,128)}, u32[]{:S(2)}) copy-start(f32[2048,32]{0,1:T(8,128)} %param.7) | copy-start | bytes 786436
  89.7 1.6 %copy-start.5 = (f32[4096,128]{1,0:T(8,128)S(1)}, f32[4096,128]{1,0:T(8,128)}, u32[]{:S(2)}) copy-start(f32[4096,128]{1,0:T(8,128)} %all-gather.3.cloned.1.call-done) | copy-start | bytes 6291460
  112.0 17.7 %all-to-all-start.4 = ((f32[32,1,256]{2,1,0:T(1,128)}), f32[32,1,256]{2,1,0:T(1,128)S(1)}, u32[]{:S(2)}, u32[]{:S(2)}) async-start(f32[32,1,256]{2,1,0:T(1,128)} %reshape.36), calls=%async_computation.4 | async-start | bytes 65536 | tf_op jit(solution)/shard_map/all_to_all | solution.py:341
  119.8 11.2 %copy-start.6 = (f32[4096,128]{1,0:T(8,128)S(1)}, f32[4096,128]{1,0:T(8,128)}, u32[]{:S(2)}) copy-start(f32[4096,128]{1,0:T(8,128)} %all-gather.3.cloned.1.call-done) | copy-start | bytes 6291460
Sparse Core Ops, SparseCore 0:
  43.5 40.4 all-gather.2

commit v3 on v2

v3 whole, which is shorter than its diff:
```python
import functools
import jax
import jax.numpy as jnp
from jax import lax
from jax.experimental import pallas as pl
from jax.experimental.pallas import tpu as pltpu
from jax.sharding import PartitionSpec as P

MOST = 64
BLOCK = 64
STEP = 8
LANES = 128
VMEM = pl.BlockSpec(memory_space=pltpu.VMEM)
HBM = pl.BlockSpec(memory_space=pltpu.HBM)
PARAMS = pltpu.CompilerParams(vmem_limit_bytes=48 * 1024 * 1024)
FETCHING = pltpu.CompilerParams(vmem_limit_bytes=60 * 1024 * 1024)


def product(left, right):
    return jnp.dot(left, right, precision=lax.Precision.HIGHEST, preferred_element_type=jnp.float32)


def dot(left, right, left_dim, right_dim):
    return lax.dot_general(
        left,
        right,
        (((left_dim,), (right_dim,)), ((), ())),
        precision=lax.Precision.HIGHEST,
        preferred_element_type=jnp.float32,
    )


def hot_dot(hot, values, hot_dim, value_dim):
    high = values.astype(jnp.bfloat16)
    rest = values - high.astype(jnp.float32)
    middle = rest.astype(jnp.bfloat16)
    low = (rest - middle.astype(jnp.float32)).astype(jnp.bfloat16)
    dims = (((hot_dim,), (value_dim,)), ((), ()))
    parts = [
        lax.dot_general(hot, piece, dims, preferred_element_type=jnp.float32)
        for piece in (high, middle, low)
    ]
    return parts[0] + parts[1] + parts[2]


def dot_hot(values, hot):
    high = values.astype(jnp.bfloat16)
    rest = values - high.astype(jnp.float32)
    middle = rest.astype(jnp.bfloat16)
    low = (rest - middle.astype(jnp.float32)).astype(jnp.bfloat16)
    parts = [
        jnp.dot(piece, hot, preferred_element_type=jnp.float32) for piece in (high, middle, low)
    ]
    return parts[0] + parts[1] + parts[2]


def cost(micros):
    return pl.CostEstimate(flops=int(micros * 1e9), bytes_accessed=0, transcendentals=0)


def iota(shape, dim):
    return lax.broadcasted_iota(jnp.int32, shape, dim)


def pack_slab(ref, cols):
    per = LANES // cols
    rows = ref.shape[0] // per
    return jnp.concatenate(
        [ref[pl.ds(p, rows, stride=per), :][:, :cols] for p in range(per)], axis=1
    )


def unpack_slab(ref, packed, cols):
    per = LANES // cols
    rows = packed.shape[0]
    for p in range(per):
        piece = jnp.concatenate(
            [packed[:, p * cols : (p + 1) * cols], jnp.zeros((rows, LANES - cols), jnp.float32)],
            axis=1,
        )
        ref[pl.ds(p, rows, stride=per), :] = piece


def pick_kernel(block_ref, row_hbm, matrix_hbm, out_ref, row_ref, matrix_ref, row_sem, sems):
    steps = sems.shape[0]
    rows, width = matrix_ref.shape
    count = row_ref.shape[1]
    chunk = rows // steps
    fetch_row = pltpu.make_async_copy(row_hbm, row_ref, row_sem)
    fetch_row.start()
    fetches = []
    for i in range(steps):
        at = pl.ds(i * chunk, chunk)
        fetch = pltpu.make_async_copy(matrix_hbm.at[at, :], matrix_ref.at[at, :], sems.at[i])
        fetch.start()
        fetches.append(fetch)
    fetch_row.wait()
    row = row_ref[...]
    owner_row = row // width
    diagonal = iota((count, count), 0) == iota((count, count), 1)
    owner_column = jnp.sum(jnp.where(diagonal, owner_row, 0), axis=1, keepdims=True)
    same = (owner_column == owner_row) & (iota((count, count), 0) < iota((count, count), 1))
    slot_row = jnp.sum(same.astype(jnp.int32), axis=0, keepdims=True)
    local_row = row - block_ref[0] * width
    by_slot = (iota((MOST, count), 0) == slot_row).astype(jnp.bfloat16)
    by_column = (iota((width, count), 0) == local_row).astype(jnp.bfloat16)
    pick = lax.dot_general(
        by_slot, by_column, (((1,), (1,)), ((), ())), preferred_element_type=jnp.float32
    ).astype(jnp.bfloat16)
    for i in range(steps):
        fetches[i].wait()
        got = hot_dot(pick, matrix_ref[i * chunk : (i + 1) * chunk, :], 1, 1)
        for piece in range(chunk // LANES):
            out_ref[i * (chunk // LANES) + piece] = got[:, piece * LANES : (piece + 1) * LANES]


def pick_columns(block, pivots, matrix, steps=2):
    rows_dev, cols_dev = matrix.shape
    count = pivots.shape[0]
    return pl.pallas_call(
        pick_kernel,
        out_shape=jax.ShapeDtypeStruct((rows_dev // LANES, MOST, LANES), jnp.float32),
        in_specs=[pl.BlockSpec(memory_space=pltpu.SMEM), HBM, HBM],
        out_specs=VMEM,
        scratch_shapes=[
            pltpu.VMEM((1, count), jnp.int32),
            pltpu.VMEM((rows_dev, cols_dev), jnp.float32),
            pltpu.SemaphoreType.DMA,
            pltpu.SemaphoreType.DMA((steps,)),
        ],
        compiler_params=FETCHING,
        cost_estimate=cost(2),
        name="pick_columns",
    )(block, pivots.reshape(1, count), matrix)


def sketch_kernel(gaussian_ref, matrix_ref, slab_ref, out_ref, trail_ref):
    pieces = out_ref.shape[0]
    width = matrix_ref.shape[1]
    cols = slab_ref.shape[0]
    gaussian = gaussian_ref[...]
    sketch = dot(gaussian, matrix_ref[...], 1, 0)
    for half in range(width // LANES):
        out_ref[:, 8 * half : 8 * half + 8, :] = sketch[
            :, half * LANES : (half + 1) * LANES
        ].reshape(pieces, 8, LANES)
    trail_ref[:, :cols] = dot(gaussian, slab_ref[...], 1, 1)
    packed = pack_slab(trail_ref, cols)
    at = 8 * (width // LANES)
    for piece in range(pieces):
        out_ref[piece, at : at + 2, :] = packed[2 * piece : 2 * piece + 2]
        out_ref[piece, at + 2 :, :] = jnp.zeros((6, LANES), jnp.float32)


def sketch_sums(gaussian, matrix, slab, pieces):
    return pl.pallas_call(
        sketch_kernel,
        out_shape=jax.ShapeDtypeStruct((pieces, 24, LANES), jnp.float32),
        in_specs=[VMEM] * 3,
        out_specs=VMEM,
        scratch_shapes=[pltpu.VMEM((gaussian.shape[0], LANES), jnp.float32)],
        compiler_params=PARAMS,
        cost_estimate=cost(4),
        name="sketch_sums",
    )(gaussian, matrix, slab)


def part_kernel(width, row_ref, spread_ref, part_ref):
    count = row_ref.shape[1]
    slots = spread_ref.shape[0]
    owner_row = row_ref[...] // width
    diagonal = iota((count, count), 0) == iota((count, count), 1)
    owner = jnp.sum(jnp.where(diagonal, owner_row, 0), axis=1, keepdims=True)
    same = (owner == owner_row) & (iota((count, count), 1) < iota((count, count), 0))
    slot = jnp.sum(same.astype(jnp.int32), axis=1, keepdims=True)
    place = (iota((count, slots), 1) == owner * MOST + slot).astype(jnp.bfloat16)
    part_ref[...] = hot_dot(place, spread_ref[...], 1, 0)


def panel_part(width, pivots, spread):
    count = pivots.shape[0]
    return pl.pallas_call(
        functools.partial(part_kernel, width),
        out_shape=jax.ShapeDtypeStruct((count, LANES), jnp.float32),
        in_specs=[VMEM, VMEM],
        out_specs=VMEM,
        compiler_params=PARAMS,
        cost_estimate=cost(1),
        name="panel_part",
    )(pivots.reshape(1, count), spread)


def gram_kernel(part_ref, sketch_ref, send_ref, gram_ref):
    half = part_ref.shape[0] // 2
    gram_ref[...] = dot(part_ref[...], part_ref[...], 1, 1)
    send_ref[:, 0:16, :] = sketch_ref[:, 0:16, :]
    send_ref[:, 28:32, :] = sketch_ref[:, 16:20, :]
    for piece in range(send_ref.shape[0]):
        low = 4 * piece
        send_ref[piece, 16:20, :] = gram_ref[low : low + 4, :half]
        send_ref[piece, 20:24, :] = gram_ref[low : low + 4, half:]
        send_ref[piece, 24:28, :] = gram_ref[half + low : half + low + 4, half:]


def gram_products(part, sketch):
    count = part.shape[0]
    pieces = sketch.shape[0]
    return pl.pallas_call(
        gram_kernel,
        out_shape=jax.ShapeDtypeStruct((pieces, 32, LANES), jnp.float32),
        in_specs=[VMEM, VMEM],
        out_specs=VMEM,
        scratch_shapes=[pltpu.VMEM((count, count), jnp.float32)],
        compiler_params=PARAMS,
        cost_estimate=cost(1),
        name="gram_products",
    )(part, sketch)


def row_sums_kernel(block_ref, row_ref, got_ref, send_ref, sketch_ref, trail_ref):
    width = sketch_ref.shape[1]
    count = row_ref.shape[1]
    total = jnp.sum(got_ref[...], axis=0)
    sketch = jnp.concatenate([total[0:8], total[8:16]], axis=1)
    sketch_ref[...] = sketch
    trail_ref[...] = total[28:30]
    local_row = row_ref[...] - block_ref[0] * width
    by_column = (iota((width, count), 0) == local_row).astype(jnp.bfloat16)
    chosen = dot_hot(sketch, by_column)
    both = jnp.concatenate([chosen[:, :LANES], chosen[:, LANES:], total[16:32]], axis=0)
    for piece in range(send_ref.shape[0]):
        send_ref[piece] = both


def row_sums(block, pivots, got, width, pieces):
    count = pivots.shape[0]
    return pl.pallas_call(
        row_sums_kernel,
        out_shape=(
            jax.ShapeDtypeStruct((pieces, 32, LANES), jnp.float32),
            jax.ShapeDtypeStruct((8, width), jnp.float32),
            jax.ShapeDtypeStruct((2, LANES), jnp.float32),
        ),
        in_specs=[pl.BlockSpec(memory_space=pltpu.SMEM), VMEM, VMEM],
        out_specs=(VMEM,) * 3,
        compiler_params=PARAMS,
        cost_estimate=cost(1),
        name="row_sums",
    )(block, pivots.reshape(1, count), got)


def col_sums_kernel(got_ref, panel_ref, slab_ref, send_ref, gauss_ref, cross_ref):
    cols = slab_ref.shape[0]
    pieces = send_ref.shape[0]
    panel = jnp.concatenate([panel_ref[k] for k in range(panel_ref.shape[0])], axis=1)
    cross_ref[:, :cols] = dot(panel, slab_ref[...], 1, 1)
    total = jnp.sum(got_ref[...], axis=0)
    gauss_ref[...] = jnp.concatenate([total[0:8], total[8:16]], axis=1)
    gram = total[16:28]
    packed = pack_slab(cross_ref, cols)
    for piece in range(pieces):
        send_ref[piece, 0:12, :] = gram
        send_ref[piece, 12:14, :] = packed[2 * piece : 2 * piece + 2]
        send_ref[piece, 14:16, :] = jnp.zeros((2, LANES), jnp.float32)


def col_sums(got, panel, slab, pieces):
    count = panel.shape[1]
    return pl.pallas_call(
        col_sums_kernel,
        out_shape=(
            jax.ShapeDtypeStruct((pieces, 16, LANES), jnp.float32),
            jax.ShapeDtypeStruct((8, count), jnp.float32),
        ),
        in_specs=[VMEM] * 3,
        out_specs=(VMEM,) * 2,
        scratch_shapes=[pltpu.VMEM((count, LANES), jnp.float32)],
        compiler_params=PARAMS,
        cost_estimate=cost(2),
        name="col_sums",
    )(got, panel, slab)


def cross_sums_kernel(got_ref, send_ref):
    total = jnp.sum(got_ref[:, 8:16, :], axis=0)[4:6]
    for piece in range(send_ref.shape[0]):
        send_ref[piece] = total


def cross_sums(got):
    pieces = got.shape[0]
    return pl.pallas_call(
        cross_sums_kernel,
        out_shape=jax.ShapeDtypeStruct((pieces, 2, LANES), jnp.float32),
        in_specs=[VMEM],
        out_specs=VMEM,
        compiler_params=PARAMS,
        cost_estimate=cost(1),
        name="cross_sums",
    )(got)


def block_inverse(block):
    n = block.shape[0]
    groups = n // 8
    sub = iota((8, 2 * n), 0)
    eye = (iota((n, n), 0) == iota((n, n), 1)).astype(jnp.float32)
    whole = jnp.concatenate([block, eye], axis=1)
    rows = [whole[8 * g : 8 * g + 8] for g in range(groups)]
    diag = [jnp.ones((8, 2 * n), jnp.float32) for _ in rows]
    for first in range(0, n, STEP):
        cols = [
            {
                g: jnp.broadcast_to(rows[g][:, j : j + 1], (8, 2 * n))
                for g in range(first // 8, groups)
            }
            for j in range(first, first + STEP)
        ]
        for t in range(STEP):
            k = first + t
            at, s = k // 8, k % 8
            col = cols[t]
            pivot = jnp.broadcast_to(col[at][s : s + 1], (8, 2 * n))
            inverse = 1.0 / pivot
            diag[at] = jnp.where(sub == s, pivot, diag[at])
            scaled = jnp.broadcast_to(rows[at][s : s + 1], (8, 2 * n)) * inverse
            for u in range(t + 1, STEP):
                other = jnp.broadcast_to(cols[u][at][s : s + 1], (8, 2 * n)) * inverse
                for g in range(at, groups):
                    cols[u][g] = cols[u][g] - col[g] * other
            for g in range(at, groups):
                factor = col[g] if g > at else jnp.where(sub > s, col[g], 0.0)
                rows[g] = rows[g] - factor * scaled
    out = jnp.concatenate([r * lax.rsqrt(d) for r, d in zip(rows, diag)], axis=0)
    return out[:, n:]


def inverse_kernel(gram_ref, out_ref, work):
    n = out_ref.shape[0]
    half = n // 2
    for piece in range(gram_ref.shape[0]):
        low = 4 * piece
        work[low : low + 4, :half] = gram_ref[piece, 0:4, :]
        work[low : low + 4, half:n] = gram_ref[piece, 4:8, :]
        work[half + low : half + low + 4, half:n] = gram_ref[piece, 8:12, :]
    work[half:, :half] = jnp.zeros((half, half), jnp.float32)
    work[:, n:] = (iota((n, n), 0) == iota((n, n), 1)).astype(jnp.float32)
    for top in range(0, n, BLOCK):
        end = top + BLOCK
        inv = block_inverse(work[top:end, top:end])
        if end == n:
            out_ref[top:end, :] = dot(inv, work[top:end, n:], 1, 0)
            break
        lo = end // LANES * LANES
        hi = -(-(n + end) // LANES) * LANES
        strip = dot(inv, work[top:end, lo:hi], 1, 0)
        done = strip[:, n - lo :]
        if hi < 2 * n:
            done = jnp.concatenate([done, jnp.zeros((BLOCK, 2 * n - hi), jnp.float32)], axis=1)
        out_ref[top:end, :] = done
        work[end:, lo:hi] -= dot(strip[:, end - lo : n - lo], strip, 0, 0)


def inverse_factor(gram, n):
    return pl.pallas_call(
        inverse_kernel,
        out_shape=jax.ShapeDtypeStruct((n, n), jnp.float32),
        in_specs=[VMEM],
        out_specs=VMEM,
        scratch_shapes=[pltpu.VMEM((n, 2 * n), jnp.float32)],
        compiler_params=PARAMS,
        cost_estimate=cost(10),
        name="inverse_factor",
    )(gram)


def finish_kernel(inv_ref, packed_ref, panel_ref, slab_ref, gauss_ref, trail_ref, coupling_ref, projected_ref, sketch_ref, cross_ref):
    cols = slab_ref.shape[0]
    inv = inv_ref[...]
    unpack_slab(cross_ref, packed_ref[...], cols)
    coupling = dot(cross_ref[:, :cols], inv, 0, 1)
    coupling_ref[...] = coupling
    weights = dot(coupling, inv, 1, 0)
    group = panel_ref.shape[0] // 2
    for low in range(0, panel_ref.shape[0], group):
        at = slice(low * LANES, (low + group) * LANES)
        panel = jnp.concatenate([panel_ref[k] for k in range(low, low + group)], axis=1)
        projected_ref[:, at] = slab_ref[:, at] - dot(weights, panel, 1, 0)
    per = LANES // cols
    trail = jnp.concatenate(
        [
            trail_ref[m : m + 1, p * cols : (p + 1) * cols]
            for m in range(trail_ref.shape[0])
            for p in range(per)
        ],
        axis=0,
    )
    sketch_ref[...] = trail - dot(gauss_ref[...], weights, 1, 1)


def finish(inv, cross, panel, slab, gauss_panel, gauss_trail):
    count = panel.shape[1]
    cols = slab.shape[0]
    return pl.pallas_call(
        finish_kernel,
        out_shape=(
            jax.ShapeDtypeStruct((cols, count), jnp.float32),
            jax.ShapeDtypeStruct(slab.shape, jnp.float32),
            jax.ShapeDtypeStruct((gauss_panel.shape[0], cols), jnp.float32),
        ),
        in_specs=[VMEM] * 6,
        out_specs=(VMEM,) * 3,
        scratch_shapes=[pltpu.VMEM((count, LANES), jnp.float32)],
        compiler_params=PARAMS,
        cost_estimate=cost(3),
        name="finish",
    )(inv, cross, panel, slab, gauss_panel, gauss_trail)


def exchange(pieces, axis):
    return lax.all_to_all(pieces, axis, 0, 0, tiled=True)


def shards(matrix, gaussian, pivots, trailing):
    rows_dev, cols_dev = matrix.shape
    count = pivots.shape[0]
    slab_cols = trailing.shape[1]
    n_rows = lax.axis_size("rows")
    n_cols = lax.axis_size("cols")
    block = lax.axis_index("cols").reshape(1)
    slab = trailing.T

    mine = pick_columns(block, pivots, matrix)
    spread = exchange(mine, "cols")
    late_gaussian, mine = lax.optimization_barrier((gaussian, mine))
    sketch_part = sketch_sums(late_gaussian, matrix, slab, n_rows)

    spread, sketch_part = lax.optimization_barrier((spread, sketch_part))
    part = panel_part(cols_dev, pivots, spread.reshape(n_cols * MOST, LANES))
    panel = lax.all_gather(part, "cols")
    send = gram_products(part, sketch_part)
    send, sketch, gauss_trail = row_sums(block, pivots, exchange(send, "rows"), cols_dev, n_cols)
    send, gauss_panel = col_sums(exchange(send, "cols"), panel, slab, n_rows)
    got = exchange(send, "rows")
    cross = exchange(cross_sums(got), "rows").reshape(-1, LANES)
    inv = inverse_factor(got, count)
    coupling, projected, trailing_sketch = finish(
        inv, cross, panel, slab, gauss_panel, gauss_trail
    )
    return (sketch, coupling.T, projected.T, trailing_sketch)


def solution(mesh):
    placed = (P("rows", "cols"), P(None, "rows"), P(), P("rows", "cols"))
    return jax.shard_map(
        shards,
        mesh=mesh,
        in_specs=placed,
        out_specs=(P("rows", "cols"), P(None, "cols"), P("rows", "cols"), P("rows", "cols")),
        check_vma=False,
    )
```

time: 141 us -> 134 us (0.950)
  local copies, waits for them, and re-layouts: 9.33 us -> 3.19 us
  Pallas kernels: 22.9 us -> 25.7 us
  blocking collectives: 63.8 us -> 61.3 us
    unnamed x24 -> x12, local copies, waits for them, and re-layouts: 8.01 us -> 3.19 us
    all_to_all x3, blocking collectives: 63.8 us -> 61.3 us  [exchange(): return lax.all_to_all(pieces, axis, 0, 0, tiled=True)]
    pallas_call x4 -> x5, Pallas kernels: 10.5 us -> 12.6 us  [the longest x1 3.59 us: pick_columns(): pl.pallas_call(pick_kernel, out_shape=jax.ShapeDtypeStruct((rows_dev // L...]
  transfers between devices with their start and end apart: 3 -> 3, of which waited for: 1 -> 1; matrix products, arithmetic and copies ran while one was open for 0% -> 0% of each run, Pallas kernels for 10% -> 12%
where the time goes in v3:
time: 134 us
  blocking collectives  61.3 us (46%)
  Pallas kernels  25.7 us (19%)
  starting transfers between devices  17.1 us (13%)
  between operations  14.1 us (11%)
  waiting for transfers between devices  12.2 us (9%)
  local copies, waits for them, and re-layouts  3.19 us (2%)
    all_to_all x3, blocking collectives, exchange(): return lax.all_to_all(pieces, axis, 0, 0, tiled=True)  61.3 us
    all_to_all x2, starting transfers between devices, exchange(): return lax.all_to_all(pieces, axis, 0, 0, tiled=True)  17 us
    all_to_all x2, waiting for transfers between devices, exchange(): return lax.all_to_all(pieces, axis, 0, 0, tiled=True)  12.2 us
    pallas_call x1, Pallas kernels, inverse_factor(): pl.pallas_call(inverse_kernel, out_shape=jax.ShapeDtypeStruct((n, n), jnp...  9.86 us
    pallas_call x1, Pallas kernels, pick_columns(): pl.pallas_call(pick_kernel, out_shape=jax.ShapeDtypeStruct((rows_dev // L...  3.59 us
    pallas_call x1, Pallas kernels, sketch_sums(): pl.pallas_call(sketch_kernel, out_shape=jax.ShapeDtypeStruct((pieces, 24,...  3.54 us
    unnamed x12, local copies, waits for them, and re-layouts  3.19 us
    pallas_call x1, Pallas kernels, finish(): pl.pallas_call(finish_kernel, out_shape=(jax.ShapeDtypeStruct((cols, coun...  2.72 us
  transfers between devices with their start and end apart: 3, of which 1 were waited for; matrix products, arithmetic and copies ran while one was open for 0% of the time, Pallas kernels for 12%

profile of v3, /device:TPU:1, one launch (start us, length us, event | category | flops | bytes accessed | tf_op | source)
XLA Modules:
  0.0 133.6 jit_solution(10956734983990647770)
XLA Ops:
  7.2 0.0 copy-start
  7.2 0.0 copy-start.4
  7.2 3.6 %pick_columns.1 = f32[16,64,128]{2,1,0:T(8,128)} custom-call(s32[1]{0:T(128)} %bitcast.block_ref, s32[1,256]{1,0:T(1,128)} %bitcast.15, f32[2048,256]{1,0:T(8,128)} %matrix_ref.1), custom_call_target="tpu_custom_call" | custom-call | flops 2000000000 | tf_op jit(solution)/shard_map/pick_columns/pallas_call | solution.py:120
  10.8 10.3 %all-to-all-start = ((f32[16,64,128]{2,1,0:T(8,128)}), f32[16,64,128]{2,1,0:T(8,128)S(1)}, u32[]{:S(2)}, u32[]{:S(2)}) async-start(f32[16,64,128]{2,1,0:T(8,128)} %pick_columns.1), calls=%async_computation | async-start | bytes 1048576 | tf_op jit(solution)/shard_map/all_to_all | solution.py:421
  21.0 0.0 all-gather.3.cloned.1.call-start
  21.1 0.0 copy-done
  21.1 0.0 copy-done.4
  21.1 0.0 copy-start.1
  21.1 1.6 %copy-done.1 = f32[256,2048]{1,0:T(8,128)S(1)} copy-done((f32[256,2048]{1,0:T(8,128)S(1)}, f32[256,2048]{1,0:T(8,128)}, u32[]{:S(2)}) %copy-start.1) | copy-done | bytes 2097176
  22.7 0.0 copy-start.5
  22.7 3.5 %sketch_sums.1.sketch_ref = f32[32,24,128]{2,1,0:T(8,128)S(1)} custom-call(f32[256,2048]{1,0:T(8,128)S(1)} %copy-done.1, f32[2048,256]{1,0:T(8,128)S(1)} %copy-done, f32[32,2048]{1,0:T(8,128)S(1)} %bitcast.12), custom_call_target="tpu_custom_call" | custom-call | flops 4000000000 | tf_op jit(solution)/shard_map/sketch_sums/pallas_call | solution.py:156
  26.2 12.1 %all-to-all-done = f32[16,64,128]{2,1,0:T(8,128)S(1)} async-done(((f32[16,64,128]{2,1,0:T(8,128)}), f32[16,64,128]{2,1,0:T(8,128)S(1)}, u32[]{:S(2)}, u32[]{:S(2)}) %all-to-all-start) | async-done | bytes 524320 | tf_op jit(solution)/shard_map/all_to_all | solution.py:421
  38.4 0.0 copy-done.5
  38.4 1.4 %panel_part.1.part_ref = f32[256,128]{1,0:T(8,128)} custom-call(s32[1,256]{1,0:T(1,128)S(1)} %bitcast.16, f32[1024,128]{1,0:T(8,128)S(1)} %bitcast.8), custom_call_target="tpu_custom_call" | custom-call | flops 1000000000 | tf_op jit(solution)/shard_map/panel_part/pallas_call | solution.py:182
  39.8 0.0 all-gather.3.cloned.1.call-update
  39.9 1.3 gram_products.1
  41.2 27.6 %all_to_all.25.got_ref = f32[32,32,128]{2,1,0:T(8,128)S(1)} all-to-all(f32[32,32,128]{2,1,0:T(8,128)S(1)} %gram_products.1), channel_id=1, replica_groups=mesh['rows'=32,'cols'=16] {'rows'}, dimensions={0} | all-to-all | bytes 1048576 | tf_op jit(solution)/shard_map/all_to_all | solution.py:421
  68.8 0.7 row_sums.1
  69.4 15.1 %all_to_all.26.got_ref = f32[16,32,128]{2,1,0:T(8,128)S(1)} all-to-all(f32[16,32,128]{2,1,0:T(8,128)S(1)} %get-tuple-element.19), channel_id=1, replica_groups=mesh['rows'=32,'cols'=16] {'cols'}, dimensions={0} | all-to-all | bytes 524288 | tf_op jit(solution)/shard_map/all_to_all | solution.py:421
  84.5 0.0 all-gather.3.cloned.1.call-done
  84.5 0.0 copy-start.2
  84.5 1.6 %copy-done.2 = f32[4096,128]{1,0:T(8,128)S(1)} copy-done((f32[4096,128]{1,0:T(8,128)S(1)}, f32[4096,128]{1,0:T(8,128)}, u32[]{:S(2)}) %copy-start.2) | copy-done | bytes 2097176
  86.1 1.9 %col_sums.1 = (f32[32,16,128]{2,1,0:T(8,128)S(1)}, f32[8,256]{1,0:T(8,128)S(1)}) custom-call(f32[16,32,128]{2,1,0:T(8,128)S(1)} %all_to_all.26.got_ref, f32[16,256,128]{2,1,0:T(8,128)S(1)} %bitcast.10, f32[32,2048]{1,0:T(8,128)S(1)} %bitcast.13), custom_call_target="tpu_custom_call" | custom-call | flops 2000000000 | tf_op jit(solution)/shard_map/col_sums/pallas_call | solution.py:269
  88.0 18.7 %all_to_all.27.gram_ref.got_ref = f32[32,16,128]{2,1,0:T(8,128)S(1)} all-to-all(f32[32,16,128]{2,1,0:T(8,128)S(1)} %get-tuple-element.20), channel_id=1, replica_groups=mesh['rows'=32,'cols'=16] {'rows'}, dimensions={0} | all-to-all | bytes 524288 | tf_op jit(solution)/shard_map/all_to_all | solution.py:421
  106.7 0.7 cross_sums.1
  107.3 6.8 %all-to-all-start.4 = ((f32[32,2,128]{2,1,0:T(2,128)}), f32[32,2,128]{2,1,0:T(2,128)S(1)}, u32[]{:S(2)}, u32[]{:S(2)}) async-start(f32[32,2,128]{2,1,0:T(2,128)} %cross_sums.1), calls=%async_computation.4 | async-start | bytes 65536 | tf_op jit(solution)/shard_map/all_to_all | solution.py:421
  114.1 0.0 copy-start.3
  114.1 9.9 %inverse_factor.1.inv_ref = f32[256,256]{1,0:T(8,128)S(1)} custom-call(f32[32,16,128]{2,1,0:T(8,128)S(1)} %all_to_all.27.gram_ref.got_ref), custom_call_target="tpu_custom_call" | custom-call | flops 10000000000 | tf_op jit(solution)/shard_map/inverse_factor/pallas_call | solution.py:365
  124.0 0.0 all-to-all-done.4
  124.0 0.0 copy-done.3
  124.0 2.7 %finish.1 = (f32[32,256]{1,0:T(8,128)}, f32[32,2048]{1,0:T(8,128)}, f32[8,32]{1,0:T(8,128)}) custom-call(f32[256,256]{1,0:T(8,128)S(1)} %inverse_factor.1.inv_ref, f32[64,128]{1,0:T(8,128)S(1)} %bitcast.9, f32[16,256,128]{2,1,0:T(8,128)S(1)} %bitcast.11, f32[32,2048]{1,0:T(8,128)S(1)} %bitcast.14, f32[8,256]{1,0:T(8,128)S(1)} %get-tuple-element.21.gauss_ref, ...), custom_call_target="tpu_custom_call" | custom-call | flops 3000000000 | tf_op jit(solution)/shard_map/finish/pallas_call | solution.py:404
Async XLA Ops:
  7.2 13.9 %copy-start = (f32[2048,256]{1,0:T(8,128)S(1)}, f32[2048,256]{1,0:T(8,128)}, u32[]{:S(2)}) copy-start(f32[2048,256]{1,0:T(8,128)} %matrix_ref.1) | copy-start | bytes 6291460
  7.2 13.9 %copy-start.4 = (f32[2048,32]{0,1:T(8,128)S(1)}, f32[2048,32]{0,1:T(8,128)}, u32[]{:S(2)}) copy-start(f32[2048,32]{0,1:T(8,128)} %param.7) | copy-start | bytes 786436
  10.8 27.6 %all-to-all-start = ((f32[16,64,128]{2,1,0:T(8,128)}), f32[16,64,128]{2,1,0:T(8,128)S(1)}, u32[]{:S(2)}, u32[]{:S(2)}) async-start(f32[16,64,128]{2,1,0:T(8,128)} %pick_columns.1), calls=%async_computation | async-start | bytes 1048576 | tf_op jit(solution)/shard_map/all_to_all | solution.py:421
  21.0 63.5 %all-gather.3.cloned.1.call-start = ((), (), s32[]{:S(2)}) async-start(), calls=%async_computation.5 | async-start | bytes 2228224 | tf_op jit(solution)/shard_map/all_gather | solution.py:440
  21.1 1.6 %copy-start.1 = (f32[256,2048]{1,0:T(8,128)S(1)}, f32[256,2048]{1,0:T(8,128)}, u32[]{:S(2)}) copy-start(f32[256,2048]{1,0:T(8,128)} %gaussian_ref) | copy-start | bytes 6291460
  22.7 15.7 %copy-start.5 = (s32[256]{0:T(256)S(1)}, s32[256]{0:T(256)}, u32[]{:S(2)}) copy-start(s32[256]{0:T(256)} %param.6) | copy-start | bytes 3076
  84.5 1.6 %copy-start.2 = (f32[4096,128]{1,0:T(8,128)S(1)}, f32[4096,128]{1,0:T(8,128)}, u32[]{:S(2)}) copy-start(f32[4096,128]{1,0:T(8,128)} %all-gather.3.cloned.1.call-done) | copy-start | bytes 6291460
  107.3 16.7 %all-to-all-start.4 = ((f32[32,2,128]{2,1,0:T(2,128)}), f32[32,2,128]{2,1,0:T(2,128)S(1)}, u32[]{:S(2)}, u32[]{:S(2)}) async-start(f32[32,2,128]{2,1,0:T(2,128)} %cross_sums.1), calls=%async_computation.4 | async-start | bytes 65536 | tf_op jit(solution)/shard_map/all_to_all | solution.py:421
  114.1 9.9 %copy-start.3 = (f32[4096,128]{1,0:T(8,128)S(1)}, f32[4096,128]{1,0:T(8,128)}, u32[]{:S(2)}) copy-start(f32[4096,128]{1,0:T(8,128)} %all-gather.3.cloned.1.call-done) | copy-start | bytes 6291460
Sparse Core Ops, SparseCore 0:
  40.0 42.2 all-gather.2

commit v4 on v3

--- a/solution.py
+++ b/solution.py
@@ -8,8 +8,9 @@
 
 MOST = 64
 BLOCK = 64
-STEP = 8
+STEP = 16
 LANES = 128
+HOPS = (0, 7, 6, 5, 4, 1, 2, 3)
 VMEM = pl.BlockSpec(memory_space=pltpu.VMEM)
 HBM = pl.BlockSpec(memory_space=pltpu.HBM)
 PARAMS = pltpu.CompilerParams(vmem_limit_bytes=48 * 1024 * 1024)
@@ -70,18 +71,7 @@
     )
 
 
-def unpack_slab(ref, packed, cols):
-    per = LANES // cols
-    rows = packed.shape[0]
-    for p in range(per):
-        piece = jnp.concatenate(
-            [packed[:, p * cols : (p + 1) * cols], jnp.zeros((rows, LANES - cols), jnp.float32)],
-            axis=1,
-        )
-        ref[pl.ds(p, rows, stride=per), :] = piece
-
-
-def pick_kernel(block_ref, row_hbm, matrix_hbm, out_ref, row_ref, matrix_ref, row_sem, sems):
+def pick_kernel(block_ref, row_hbm, matrix_hbm, slab_hbm, out_ref, row_ref, matrix_ref, slab_ref, row_sem, slab_sem, sems):
     steps = sems.shape[0]
     rows, width = matrix_ref.shape
     count = row_ref.shape[1]
@@ -94,6 +84,8 @@
         fetch = pltpu.make_async_copy(matrix_hbm.at[at, :], matrix_ref.at[at, :], sems.at[i])
         fetch.start()
         fetches.append(fetch)
+    fetch_slab = pltpu.make_async_copy(slab_hbm, slab_ref, slab_sem)
+    fetch_slab.start()
     fetch_row.wait()
     row = row_ref[...]
     owner_row = row // width
@@ -111,27 +103,36 @@
         fetches[i].wait()
         got = hot_dot(pick, matrix_ref[i * chunk : (i + 1) * chunk, :], 1, 1)
         for piece in range(chunk // LANES):
-            out_ref[i * (chunk // LANES) + piece] = got[:, piece * LANES : (piece + 1) * LANES]
-
-
-def pick_columns(block, pivots, matrix, steps=2):
+            out_ref[i * (chunk // LANES) + piece, :MOST, :] = got[
+                :, piece * LANES : (piece + 1) * LANES
+            ]
+    fetch_slab.wait()
+    for piece in range(rows // LANES):
+        out_ref[piece, MOST:, :] = slab_ref[:, piece * LANES : (piece + 1) * LANES]
+
+
+def pick_columns(block, pivots, matrix, slab, steps=2):
     rows_dev, cols_dev = matrix.shape
     count = pivots.shape[0]
     return pl.pallas_call(
         pick_kernel,
-        out_shape=jax.ShapeDtypeStruct((rows_dev // LANES, MOST, LANES), jnp.float32),
-        in_specs=[pl.BlockSpec(memory_space=pltpu.SMEM), HBM, HBM],
+        out_shape=jax.ShapeDtypeStruct(
+            (rows_dev // LANES, MOST + slab.shape[0], LANES), jnp.float32
+        ),
+        in_specs=[pl.BlockSpec(memory_space=pltpu.SMEM), HBM, HBM, HBM],
         out_specs=VMEM,
         scratch_shapes=[
             pltpu.VMEM((1, count), jnp.int32),
             pltpu.VMEM((rows_dev, cols_dev), jnp.float32),
+            pltpu.VMEM(slab.shape, jnp.float32),
+            pltpu.SemaphoreType.DMA,
             pltpu.SemaphoreType.DMA,
             pltpu.SemaphoreType.DMA((steps,)),
         ],
         compiler_params=FETCHING,
         cost_estimate=cost(2),
         name="pick_columns",
-    )(block, pivots.reshape(1, count), matrix)
+    )(block, pivots.reshape(1, count), matrix, slab)
 
 
 def sketch_kernel(gaussian_ref, matrix_ref, slab_ref, out_ref, trail_ref):
@@ -165,56 +166,57 @@
     )(gaussian, matrix, slab)
 
 
-def part_kernel(width, row_ref, spread_ref, part_ref):
+def part_kernel(width, row_ref, spread_ref, sketch_ref, part_ref, send_ref, gram_ref, cross_ref):
     count = row_ref.shape[1]
-    slots = spread_ref.shape[0]
+    half = count // 2
+    blocks = spread_ref.shape[0]
+    cols = spread_ref.shape[1] - MOST
+    pieces = send_ref.shape[0]
     owner_row = row_ref[...] // width
     diagonal = iota((count, count), 0) == iota((count, count), 1)
     owner = jnp.sum(jnp.where(diagonal, owner_row, 0), axis=1, keepdims=True)
     same = (owner == owner_row) & (iota((count, count), 1) < iota((count, count), 0))
     slot = jnp.sum(same.astype(jnp.int32), axis=1, keepdims=True)
-    place = (iota((count, slots), 1) == owner * MOST + slot).astype(jnp.bfloat16)
-    part_ref[...] = hot_dot(place, spread_ref[...], 1, 0)
-
-
-def panel_part(width, pivots, spread):
-    count = pivots.shape[0]
-    return pl.pallas_call(
-        functools.partial(part_kernel, width),
-        out_shape=jax.ShapeDtypeStruct((count, LANES), jnp.float32),
-        in_specs=[VMEM, VMEM],
-        out_specs=VMEM,
-        compiler_params=PARAMS,
-        cost_estimate=cost(1),
-        name="panel_part",
-    )(pivots.reshape(1, count), spread)
-
-
-def gram_kernel(part_ref, sketch_ref, send_ref, gram_ref):
-    half = part_ref.shape[0] // 2
-    gram_ref[...] = dot(part_ref[...], part_ref[...], 1, 1)
+    place = (iota((count, blocks * MOST), 1) == owner * MOST + slot).astype(jnp.bfloat16)
+    spread = jnp.concatenate([spread_ref[b, :MOST, :] for b in range(blocks)], axis=0)
+    slab = jnp.concatenate([spread_ref[b, MOST:, :] for b in range(blocks)], axis=0)
+    part = hot_dot(place, spread, 1, 0)
+    part_ref[...] = part
+    gram_ref[...] = dot(part, part, 1, 1)
+    cross_ref[0] = dot(slab, part[:half], 1, 1)
+    cross_ref[1] = dot(slab, part[half:], 1, 1)
     send_ref[:, 0:16, :] = sketch_ref[:, 0:16, :]
     send_ref[:, 28:32, :] = sketch_ref[:, 16:20, :]
-    for piece in range(send_ref.shape[0]):
+    for piece in range(pieces):
         low = 4 * piece
         send_ref[piece, 16:20, :] = gram_ref[low : low + 4, :half]
         send_ref[piece, 20:24, :] = gram_ref[low : low + 4, half:]
         send_ref[piece, 24:28, :] = gram_ref[half + low : half + low + 4, half:]
-
-
-def gram_products(part, sketch):
-    count = part.shape[0]
+        send_ref[piece, 32:48, :] = cross_ref[0, pl.ds(piece, blocks, stride=cols), :]
+        send_ref[piece, 48:64, :] = cross_ref[1, pl.ds(piece, blocks, stride=cols), :]
+
+
+def part_products(width, pivots, spread, sketch):
+    count = pivots.shape[0]
     pieces = sketch.shape[0]
-    return pl.pallas_call(
-        gram_kernel,
-        out_shape=jax.ShapeDtypeStruct((pieces, 32, LANES), jnp.float32),
-        in_specs=[VMEM, VMEM],
-        out_specs=VMEM,
-        scratch_shapes=[pltpu.VMEM((count, count), jnp.float32)],
-        compiler_params=PARAMS,
-        cost_estimate=cost(1),
-        name="gram_products",
-    )(part, sketch)
+    blocks = spread.shape[0]
+    cols = spread.shape[1] - MOST
+    return pl.pallas_call(
+        functools.partial(part_kernel, width),
+        out_shape=(
+            jax.ShapeDtypeStruct((count, LANES), jnp.float32),
+            jax.ShapeDtypeStruct((pieces, 64, LANES), jnp.float32),
+        ),
+        in_specs=[VMEM] * 3,
+        out_specs=(VMEM,) * 2,
+        scratch_shapes=[
+            pltpu.VMEM((count, count), jnp.float32),
+            pltpu.VMEM((2, blocks * cols, LANES), jnp.float32),
+        ],
+        compiler_params=PARAMS,
+        cost_estimate=cost(3),
+        name="part_products",
+    )(pivots.reshape(1, count), spread, sketch)
 
 
 def row_sums_kernel(block_ref, row_ref, got_ref, send_ref, sketch_ref, trail_ref):
@@ -230,6 +232,8 @@
     both = jnp.concatenate([chosen[:, :LANES], chosen[:, LANES:], total[16:32]], axis=0)
     for piece in range(send_ref.shape[0]):
         send_ref[piece] = both
+        send_ref[piece, 28:29, :] = total[32 + piece : 33 + piece]
+        send_ref[piece, 29:30, :] = total[48 + piece : 49 + piece]
 
 
 def row_sums(block, pivots, got, width, pieces):
@@ -249,54 +253,25 @@
     )(block, pivots.reshape(1, count), got)
 
 
-def col_sums_kernel(got_ref, panel_ref, slab_ref, send_ref, gauss_ref, cross_ref):
-    cols = slab_ref.shape[0]
-    pieces = send_ref.shape[0]
-    panel = jnp.concatenate([panel_ref[k] for k in range(panel_ref.shape[0])], axis=1)
-    cross_ref[:, :cols] = dot(panel, slab_ref[...], 1, 1)
+def col_sums_kernel(got_ref, send_ref, gauss_ref):
     total = jnp.sum(got_ref[...], axis=0)
     gauss_ref[...] = jnp.concatenate([total[0:8], total[8:16]], axis=1)
-    gram = total[16:28]
-    packed = pack_slab(cross_ref, cols)
-    for piece in range(pieces):
-        send_ref[piece, 0:12, :] = gram
-        send_ref[piece, 12:14, :] = packed[2 * piece : 2 * piece + 2]
-        send_ref[piece, 14:16, :] = jnp.zeros((2, LANES), jnp.float32)
-
-
-def col_sums(got, panel, slab, pieces):
-    count = panel.shape[1]
+    for piece in range(send_ref.shape[0]):
+        send_ref[piece] = total[16:32]
+
+
+def col_sums(got, pieces):
     return pl.pallas_call(
         col_sums_kernel,
         out_shape=(
             jax.ShapeDtypeStruct((pieces, 16, LANES), jnp.float32),
-            jax.ShapeDtypeStruct((8, count), jnp.float32),
+            jax.ShapeDtypeStruct((8, 2 * LANES), jnp.float32),
         ),
-        in_specs=[VMEM] * 3,
+        in_specs=[VMEM],
         out_specs=(VMEM,) * 2,
-        scratch_shapes=[pltpu.VMEM((count, LANES), jnp.float32)],
-        compiler_params=PARAMS,
-        cost_estimate=cost(2),
+        compiler_params=PARAMS,
+        cost_estimate=cost(1),
         name="col_sums",
-    )(got, panel, slab)
-
-
-def cross_sums_kernel(got_ref, send_ref):
-    total = jnp.sum(got_ref[:, 8:16, :], axis=0)[4:6]
-    for piece in range(send_ref.shape[0]):
-        send_ref[piece] = total
-
-
-def cross_sums(got):
-    pieces = got.shape[0]
-    return pl.pallas_call(
-        cross_sums_kernel,
-        out_shape=jax.ShapeDtypeStruct((pieces, 2, LANES), jnp.float32),
-        in_specs=[VMEM],
-        out_specs=VMEM,
-        compiler_params=PARAMS,
-        cost_estimate=cost(1),
-        name="cross_sums",
     )(got)
 
 
@@ -374,18 +349,27 @@
     )(gram)
 
 
-def finish_kernel(inv_ref, packed_ref, panel_ref, slab_ref, gauss_ref, trail_ref, coupling_ref, projected_ref, sketch_ref, cross_ref):
+def finish_kernel(block_ref, inv_ref, got_ref, near_ref, far_ref, slab_ref, gauss_ref, trail_ref, coupling_ref, projected_ref, sketch_ref):
     cols = slab_ref.shape[0]
+    chips = near_ref.shape[0]
     inv = inv_ref[...]
-    unpack_slab(cross_ref, packed_ref[...], cols)
-    coupling = dot(cross_ref[:, :cols], inv, 0, 1)
+    cross = jnp.concatenate(
+        [
+            jnp.concatenate([got_ref[r, 12:13, :], got_ref[r, 13:14, :]], axis=1)
+            for r in range(cols)
+        ],
+        axis=0,
+    )
+    coupling = dot(cross, inv, 1, 1)
     coupling_ref[...] = coupling
     weights = dot(coupling, inv, 1, 0)
-    group = panel_ref.shape[0] // 2
-    for low in range(0, panel_ref.shape[0], group):
-        at = slice(low * LANES, (low + group) * LANES)
-        panel = jnp.concatenate([panel_ref[k] for k in range(low, low + group)], axis=1)
-        projected_ref[:, at] = slab_ref[:, at] - dot(weights, panel, 1, 0)
+    core = lax.rem(block_ref[0], 2)
+    chip = lax.div(block_ref[0], 2)
+    for step, hops in enumerate(HOPS):
+        source = lax.rem(chip + hops, chips)
+        for ref, owner in ((near_ref, 2 * source + core), (far_ref, 2 * source + 1 - core)):
+            at = pl.ds(pl.multiple_of(owner * LANES, LANES), LANES)
+            projected_ref[:, at] = slab_ref[:, at] - dot(weights, ref[step], 1, 0)
     per = LANES // cols
     trail = jnp.concatenate(
         [
@@ -398,8 +382,8 @@
     sketch_ref[...] = trail - dot(gauss_ref[...], weights, 1, 1)
 
 
-def finish(inv, cross, panel, slab, gauss_panel, gauss_trail):
-    count = panel.shape[1]
+def finish(block, inv, got, near, far, slab, gauss_panel, gauss_trail):
+    count = inv.shape[0]
     cols = slab.shape[0]
     return pl.pallas_call(
         finish_kernel,
@@ -408,44 +392,63 @@
             jax.ShapeDtypeStruct(slab.shape, jnp.float32),
             jax.ShapeDtypeStruct((gauss_panel.shape[0], cols), jnp.float32),
         ),
-        in_specs=[VMEM] * 6,
+        in_specs=[pl.BlockSpec(memory_space=pltpu.SMEM)] + [VMEM] * 7,
         out_specs=(VMEM,) * 3,
-        scratch_shapes=[pltpu.VMEM((count, LANES), jnp.float32)],
         compiler_params=PARAMS,
         cost_estimate=cost(3),
         name="finish",
-    )(inv, cross, panel, slab, gauss_panel, gauss_trail)
+    )(block, inv, got, near, far, slab, gauss_panel, gauss_trail)
 
 
 def exchange(pieces, axis):
     return lax.all_to_all(pieces, axis, 0, 0, tiled=True)
+
+
+def pass_on(value, chips):
+    n = lax.axis_size("cols")
+    return lax.ppermute(value, "cols", [(i, (i + 2 * chips) % n) for i in range(n)])
+
+
+def swap_cores(value):
+    n = lax.axis_size("cols")
+    return lax.ppermute(value, "cols", [(i, i ^ 1) for i in range(n)])
 
 
 def shards(matrix, gaussian, pivots, trailing):
     rows_dev, cols_dev = matrix.shape
     count = pivots.shape[0]
-    slab_cols = trailing.shape[1]
     n_rows = lax.axis_size("rows")
     n_cols = lax.axis_size("cols")
     block = lax.axis_index("cols").reshape(1)
     slab = trailing.T
 
-    mine = pick_columns(block, pivots, matrix)
+    mine = pick_columns(block, pivots, matrix, slab)
     spread = exchange(mine, "cols")
     late_gaussian, mine = lax.optimization_barrier((gaussian, mine))
     sketch_part = sketch_sums(late_gaussian, matrix, slab, n_rows)
-
     spread, sketch_part = lax.optimization_barrier((spread, sketch_part))
-    part = panel_part(cols_dev, pivots, spread.reshape(n_cols * MOST, LANES))
-    panel = lax.all_gather(part, "cols")
-    send = gram_products(part, sketch_part)
-    send, sketch, gauss_trail = row_sums(block, pivots, exchange(send, "rows"), cols_dev, n_cols)
-    send, gauss_panel = col_sums(exchange(send, "cols"), panel, slab, n_rows)
+    part, send = part_products(cols_dev, pivots, spread, sketch_part)
+
     got = exchange(send, "rows")
-    cross = exchange(cross_sums(got), "rows").reshape(-1, LANES)
+    part, _ = lax.optimization_barrier((part, send))
+    up, down = [part], [part]
+    for _ in range(2):
+        up.append(pass_on(up[-1], 1))
+        down.append(pass_on(down[-1], -1))
+    opposite = pass_on(part, 4)
+    got, up[2], down[2] = lax.optimization_barrier((got, up[2], down[2]))
+    send, sketch, gauss_trail = row_sums(block, pivots, got, cols_dev, n_cols)
+    got = exchange(send, "cols")
+    up.append(pass_on(up[2], 1))
+    down.append(pass_on(down[2], -1))
+    send, gauss_panel = col_sums(got, n_rows)
+    got = exchange(send, "rows")
+    near = jnp.stack(up + [opposite] + down[1:])
+    near, _ = lax.optimization_barrier((near, send))
+    far = swap_cores(near)
     inv = inverse_factor(got, count)
     coupling, projected, trailing_sketch = finish(
-        inv, cross, panel, slab, gauss_panel, gauss_trail
+        block, inv, got, near, far, slab, gauss_panel, gauss_trail
     )
     return (sketch, coupling.T, projected.T, trailing_sketch)
 

time: 134 us -> 127 us (0.948); the launches traced: 134 us -> 125 us
  blocking collectives: 61.3 us -> 0 us
  starting transfers between devices: 17.1 us -> 56.8 us
  waiting for transfers between devices: 12.2 us -> 40 us
  between operations: 14.1 us -> 0.88 us
  Pallas kernels: 25.7 us -> 23.5 us
    all_to_all x3 -> x0, blocking collectives: 61.3 us -> none  [exchange(): return lax.all_to_all(pieces, axis, 0, 0, tiled=True)]
    ppermute x0 -> x8, starting transfers between devices: none -> 25.9 us  [the longest x7 22.6 us: pass_on(): lax.ppermute(value, 'cols', [(i, (i + 2 * chips) % n) for i in range(n)])]
    all_to_all x2 -> x4, waiting for transfers between devices: 12.2 us -> 31 us  [exchange(): return lax.all_to_all(pieces, axis, 0, 0, tiled=True)]
    all_to_all x2 -> x4, starting transfers between devices: 17 us -> 30.9 us  [exchange(): return lax.all_to_all(pieces, axis, 0, 0, tiled=True)]
    ppermute x0 -> x8, waiting for transfers between devices: none -> 9 us  [the longest x7 9 us: pass_on(): lax.ppermute(value, 'cols', [(i, (i + 2 * chips) % n) for i in range(n)])]
    pallas_call x3 -> x1, Pallas kernels: 3.43 us -> 3.18 us  [part_products(): pl.pallas_call(functools.partial(part_kernel, width), out_shape=(jax.Shap...]
    unnamed x12 -> x19, local copies, waits for them, and re-layouts: 3.19 us -> 3.44 us
  transfers between devices with their start and end apart: 3 -> 12, of which waited for: 1 -> 5; matrix products, arithmetic and copies ran while one was open for 0% -> 0% of each run, Pallas kernels for 12% -> 11%
where the time goes in v4:
time: 127 us; the launch traced here: 125 us
  starting transfers between devices  56.8 us (45%)
  waiting for transfers between devices  40 us (31%)
  Pallas kernels  23.5 us (19%)
  local copies, waits for them, and re-layouts  3.45 us (3%)
    all_to_all x4, waiting for transfers between devices, exchange(): return lax.all_to_all(pieces, axis, 0, 0, tiled=True)  31 us
    all_to_all x4, starting transfers between devices, exchange(): return lax.all_to_all(pieces, axis, 0, 0, tiled=True)  30.9 us
    ppermute x7, starting transfers between devices, pass_on(): lax.ppermute(value, 'cols', [(i, (i + 2 * chips) % n) for i in range(n)])  22.6 us
    ppermute x7, waiting for transfers between devices, pass_on(): lax.ppermute(value, 'cols', [(i, (i + 2 * chips) % n) for i in range(n)])  9 us
    pallas_call x1, Pallas kernels, inverse_factor(): pl.pallas_call(inverse_kernel, out_shape=jax.ShapeDtypeStruct((n, n), jnp...  8.86 us
    pallas_call x1, Pallas kernels, pick_columns(): pl.pallas_call(pick_kernel, out_shape=jax.ShapeDtypeStruct((rows_dev // L...  3.65 us
    pallas_call x1, Pallas kernels, sketch_sums(): pl.pallas_call(sketch_kernel, out_shape=jax.ShapeDtypeStruct((pieces, 24,...  3.54 us
    unnamed x19, local copies, waits for them, and re-layouts  3.44 us
  transfers between devices with their start and end apart: 12, of which 5 were waited for; matrix products, arithmetic and copies ran while one was open for 0% of the time, Pallas kernels for 11%

profile of v4, /device:TPU:1, one launch (start us, length us, event | category | flops | bytes accessed | tf_op | source)
XLA Modules:
  0.0 124.7 jit_solution(5186608189152348963)
XLA Ops:
  0.6 0.0 copy-start
  0.6 0.0 copy-start.2
  0.7 3.7 %pick_columns.1 = f32[16,96,128]{2,1,0:T(8,128)} custom-call(s32[1]{0:T(128)} %bitcast.block_ref, s32[1,256]{1,0:T(1,128)} %bitcast.24, f32[2048,256]{1,0:T(8,128)} %matrix_ref.1, f32[32,2048]{1,0:T(8,128)} %bitcast.21), custom_call_target="tpu_custom_call" | custom-call | flops 2000000000 | tf_op jit(solution)/shard_map/pick_columns/pallas_call | solution.py:117
  4.3 10.3 %all-to-all-start = ((f32[16,96,128]{2,1,0:T(8,128)}), f32[16,96,128]{2,1,0:T(8,128)S(1)}, u32[]{:S(2)}, u32[]{:S(2)}) async-start(f32[16,96,128]{2,1,0:T(8,128)} %pick_columns.1), calls=%async_computation | async-start | bytes 1572864 | tf_op jit(solution)/shard_map/all_to_all | solution.py:404
  14.6 0.0 copy-done
  14.6 0.0 copy-done.2
  14.6 0.0 copy-start.1
  14.6 1.6 %copy-done.1 = f32[256,2048]{1,0:T(8,128)S(1)} copy-done((f32[256,2048]{1,0:T(8,128)S(1)}, f32[256,2048]{1,0:T(8,128)}, u32[]{:S(2)}) %copy-start.1) | copy-done | bytes 2097176
  16.2 0.0 copy-start.3
  16.2 3.5 %sketch_sums.1.sketch_ref = f32[32,24,128]{2,1,0:T(8,128)S(1)} custom-call(f32[256,2048]{1,0:T(8,128)S(1)} %copy-done.1, f32[2048,256]{1,0:T(8,128)S(1)} %copy-done, f32[32,2048]{1,0:T(8,128)S(1)} %bitcast.22), custom_call_target="tpu_custom_call" | custom-call | flops 4000000000 | tf_op jit(solution)/shard_map/sketch_sums/pallas_call | solution.py:157
  19.8 0.0 copy-start.4
  19.8 0.8 copy-done.4
  20.5 16.8 %all-to-all-done.spread_ref = f32[16,96,128]{2,1,0:T(8,128)S(1)} async-done(((f32[16,96,128]{2,1,0:T(8,128)}), f32[16,96,128]{2,1,0:T(8,128)S(1)}, u32[]{:S(2)}, u32[]{:S(2)}) %all-to-all-start) | async-done | bytes 786464 | tf_op jit(solution)/shard_map/all_to_all | solution.py:404
  37.3 0.0 copy-done.3
  37.3 0.0 copy-start.5
  37.3 1.0 copy-done.5
  38.3 3.2 %part_products.1 = (f32[256,128]{1,0:T(8,128)S(1)}, f32[32,64,128]{2,1,0:T(8,128)}) custom-call(s32[1,256]{1,0:T(1,128)S(1)} %bitcast.25, f32[16,96,128]{2,1,0:T(8,128)S(1)} %all-to-all-done.spread_ref, f32[32,24,128]{2,1,0:T(8,128)S(1)} %copy-done.5), custom_call_target="tpu_custom_call" | custom-call | flops 3000000000 | tf_op jit(solution)/shard_map/part_products/pallas_call | solution.py:204
  41.5 11.2 %all-to-all-start.1 = ((f32[32,64,128]{2,1,0:T(8,128)}), f32[32,64,128]{2,1,0:T(8,128)S(1)}, u32[]{:S(2)}, u32[]{:S(2)}) async-start(f32[32,64,128]{2,1,0:T(8,128)} %get-tuple-element.25), calls=%async_computation.1 | async-start | bytes 2097152 | tf_op jit(solution)/shard_map/all_to_all | solution.py:404
  52.7 1.9 %collective-permute-start = (f32[256,128]{1,0:T(8,128)S(1)}, f32[256,128]{1,0:T(8,128)S(1)}, u32[]{:S(2)}, u32[]{:S(2)}) collective-permute-start(f32[256,128]{1,0:T(8,128)S(1)} %get-tuple-element.26), channel_id=1, source_target_pairs={{0,2},{1,3},{2,4},{3,5},{4,6},{5,7},{6,8},{7,9},{8,10},{9,11},{10,... | collective-permute-start | bytes 393224 | tf_op jit(solution)/shard_map/ppermute | solution.py:409
  54.6 4.6 %collective-permute-start.2 = (f32[256,128]{1,0:T(8,128)S(1)}, f32[256,128]{1,0:T(8,128)S(1)}, u32[]{:S(2)}, u32[]{:S(2)}) collective-permute-start(f32[256,128]{1,0:T(8,128)S(1)} %get-tuple-element.26), channel_id=1, source_target_pairs={{0,14},{1,15},{2,0},{3,1},{4,2},{5,3},{6,4},{7,5},{8,6},{9,7},{10,... | collective-permute-start | bytes 393224 | tf_op jit(solution)/shard_map/ppermute | solution.py:409
  59.2 3.1 %collective-permute-start.5 = (f32[256,128]{1,0:T(8,128)S(1)}, f32[256,128]{1,0:T(8,128)S(1)}, u32[]{:S(2)}, u32[]{:S(2)}) collective-permute-start(f32[256,128]{1,0:T(8,128)S(1)} %get-tuple-element.26), channel_id=1, source_target_pairs={{0,8},{1,9},{2,10},{3,11},{4,12},{5,13},{6,14},{7,15},{8,0},{9,1},... | collective-permute-start | bytes 393224 | tf_op jit(solution)/shard_map/ppermute | solution.py:409
  62.3 0.0 collective-permute-done
  62.4 1.9 %collective-permute-start.1 = (f32[256,128]{1,0:T(8,128)S(1)}, f32[256,128]{1,0:T(8,128)S(1)}, u32[]{:S(2)}, u32[]{:S(2)}) collective-permute-start(f32[256,128]{1,0:T(8,128)S(1)} %collective-permute-done), channel_id=1, source_target_pairs={{0,2},{1,3},{2,4},{3,5},{4,6},{5,7},{6,8},{7,9},{8,10},{9,11},{10,... | collective-permute-start | bytes 393224 | tf_op jit(solution)/shard_map/ppermute | solution.py:409
  64.3 0.0 collective-permute-done.2
  64.3 4.6 %collective-permute-start.3 = (f32[256,128]{1,0:T(8,128)S(1)}, f32[256,128]{1,0:T(8,128)S(1)}, u32[]{:S(2)}, u32[]{:S(2)}) collective-permute-start(f32[256,128]{1,0:T(8,128)S(1)} %collective-permute-done.2), channel_id=1, source_target_pairs={{0,14},{1,15},{2,0},{3,1},{4,2},{5,3},{6,4},{7,5},{8,6},{9,7},{10,... | collective-permute-start | bytes 393224 | tf_op jit(solution)/shard_map/ppermute | solution.py:409
  68.9 3.6 %collective-permute-done.1 = f32[256,128]{1,0:T(8,128)S(1)} collective-permute-done((f32[256,128]{1,0:T(8,128)S(1)}, f32[256,128]{1,0:T(8,128)S(1)}, u32[]{:S(2)}, u32[]{:S(2)}) %collective-permute-start.1) | collective-permute-done | bytes 131104 | tf_op jit(solution)/shard_map/ppermute | solution.py:409
  72.5 0.0 collective-permute-done.3
  72.5 7.9 %all-to-all-done.1.got_ref = f32[32,64,128]{2,1,0:T(8,128)S(1)} async-done(((f32[32,64,128]{2,1,0:T(8,128)}), f32[32,64,128]{2,1,0:T(8,128)S(1)}, u32[]{:S(2)}, u32[]{:S(2)}) %all-to-all-start.1) | async-done | bytes 1048608 | tf_op jit(solution)/shard_map/all_to_all | solution.py:404
  80.4 0.9 row_sums.1
  81.3 4.6 %all-to-all-start.2 = ((f32[16,32,128]{2,1,0:T(8,128)}), f32[16,32,128]{2,1,0:T(8,128)S(1)}, u32[]{:S(2)}, u32[]{:S(2)}) async-start(f32[16,32,128]{2,1,0:T(8,128)} %get-tuple-element.29), calls=%async_computation.2 | async-start | bytes 524288 | tf_op jit(solution)/shard_map/all_to_all | solution.py:404
  85.9 3.3 %collective-permute-start.4 = (f32[256,128]{1,0:T(8,128)S(1)}, f32[256,128]{1,0:T(8,128)S(1)}, u32[]{:S(2)}, u32[]{:S(2)}) collective-permute-start(f32[256,128]{1,0:T(8,128)S(1)} %collective-permute-done.1), channel_id=1, source_target_pairs={{0,2},{1,3},{2,4},{3,5},{4,6},{5,7},{6,8},{7,9},{8,10},{9,11},{10,... | collective-permute-start | bytes 393224 | tf_op jit(solution)/shard_map/ppermute | solution.py:409
  89.2 3.2 %collective-permute-start.6 = (f32[256,128]{1,0:T(8,128)S(1)}, f32[256,128]{1,0:T(8,128)S(1)}, u32[]{:S(2)}, u32[]{:S(2)}) collective-permute-start(f32[256,128]{1,0:T(8,128)S(1)} %collective-permute-done.3), channel_id=1, source_target_pairs={{0,14},{1,15},{2,0},{3,1},{4,2},{5,3},{6,4},{7,5},{8,6},{9,7},{10,... | collective-permute-start | bytes 393224 | tf_op jit(solution)/shard_map/ppermute | solution.py:409
  92.5 5.4 %collective-permute-done.4 = f32[256,128]{1,0:T(8,128)S(1)} collective-permute-done((f32[256,128]{1,0:T(8,128)S(1)}, f32[256,128]{1,0:T(8,128)S(1)}, u32[]{:S(2)}, u32[]{:S(2)}) %collective-permute-start.4) | collective-permute-done | bytes 131104 | tf_op jit(solution)/shard_map/ppermute | solution.py:409
  97.9 0.0 collective-permute-done.5
  98.0 0.0 all-to-all-done.2.got_ref
  98.0 0.7 col_sums.1
  98.7 4.8 %all-to-all-start.3 = ((f32[32,16,128]{2,1,0:T(8,128)}), f32[32,16,128]{2,1,0:T(8,128)S(1)}, u32[]{:S(2)}, u32[]{:S(2)}) async-start(f32[32,16,128]{2,1,0:T(8,128)} %get-tuple-element.30), calls=%async_computation.3 | async-start | bytes 524288 | tf_op jit(solution)/shard_map/all_to_all | solution.py:404
  103.6 0.0 collective-permute-done.6
  103.6 3.3 %collective-permute-start.7 = (f32[8,256,128]{2,1,0:T(8,128)S(1)}, f32[8,256,128]{2,1,0:T(8,128)S(1)}, u32[]{:S(2)}, u32[]{:S(2)}) collective-permute-start(f32[8,256,128]{2,1,0:T(8,128)S(1)} %bitcast_dynamic-update-slice_fusion.near_ref), channel_id=1, source_target_pairs={{0,1},{1,0},{2,3},{3,2},{4,5},{5,4},{6,7},{7,6},{8,9},{9,8},{10,11... | collective-permute-start | bytes 3145736 | tf_op jit(solution)/shard_map/ppermute | solution.py:414
  106.9 6.3 %all-to-all-done.3.gram_ref.got_ref = f32[32,16,128]{2,1,0:T(8,128)S(1)} async-done(((f32[32,16,128]{2,1,0:T(8,128)}), f32[32,16,128]{2,1,0:T(8,128)S(1)}, u32[]{:S(2)}, u32[]{:S(2)}) %all-to-all-start.3) | async-done | bytes 262176 | tf_op jit(solution)/shard_map/all_to_all | solution.py:404
  113.2 8.9 %inverse_factor.1.inv_ref = f32[256,256]{1,0:T(8,128)S(1)} custom-call(f32[32,16,128]{2,1,0:T(8,128)S(1)} %all-to-all-done.3.gram_ref.got_ref), custom_call_target="tpu_custom_call" | custom-call | flops 10000000000 | tf_op jit(solution)/shard_map/inverse_factor/pallas_call | solution.py:340
  122.1 0.0 collective-permute-done.7.far_ref
  122.1 2.6 %finish.1 = (f32[32,256]{1,0:T(8,128)}, f32[32,2048]{1,0:T(8,128)}, f32[8,32]{1,0:T(8,128)}) custom-call(s32[1]{0:T(128)} %bitcast.block_ref, f32[256,256]{1,0:T(8,128)S(1)} %inverse_factor.1.inv_ref, f32[32,16,128]{2,1,0:T(8,128)S(1)} %all-to-all-done.3.gram_ref.got_ref, f32[8,256,128]{2,1,0:T(8,128)S(1)} %bitcast_dynamic-update-slice_fusion.near_ref, ...), custom_call_target="tpu_custom_call" | custom-call | flops 3000000000 | tf_op jit(solution)/shard_map/finish/pallas_call | solution.py:388
  (8 shorter events, 0.1 us)
Async XLA Ops:
  0.6 14.0 %copy-start = (f32[2048,256]{1,0:T(8,128)S(1)}, f32[2048,256]{1,0:T(8,128)}, u32[]{:S(2)}) copy-start(f32[2048,256]{1,0:T(8,128)} %matrix_ref.1) | copy-start | bytes 6291460
  0.6 14.0 %copy-start.2 = (f32[2048,32]{0,1:T(8,128)S(1)}, f32[2048,32]{0,1:T(8,128)}, u32[]{:S(2)}) copy-start(f32[2048,32]{0,1:T(8,128)} %param.7) | copy-start | bytes 786436
  4.3 33.0 %all-to-all-start = ((f32[16,96,128]{2,1,0:T(8,128)}), f32[16,96,128]{2,1,0:T(8,128)S(1)}, u32[]{:S(2)}, u32[]{:S(2)}) async-start(f32[16,96,128]{2,1,0:T(8,128)} %pick_columns.1), calls=%async_computation | async-start | bytes 1572864 | tf_op jit(solution)/shard_map/all_to_all | solution.py:404
  14.6 1.6 %copy-start.1 = (f32[256,2048]{1,0:T(8,128)S(1)}, f32[256,2048]{1,0:T(8,128)}, u32[]{:S(2)}) copy-start(f32[256,2048]{1,0:T(8,128)} %gaussian_ref) | copy-start | bytes 6291460
  16.2 21.1 %copy-start.3 = (s32[256]{0:T(256)S(1)}, s32[256]{0:T(256)}, u32[]{:S(2)}) copy-start(s32[256]{0:T(256)} %param.6) | copy-start | bytes 3076
  19.8 0.8 copy-start.4
  37.3 1.0 copy-start.5
  41.5 38.9 %all-to-all-start.1 = ((f32[32,64,128]{2,1,0:T(8,128)}), f32[32,64,128]{2,1,0:T(8,128)S(1)}, u32[]{:S(2)}, u32[]{:S(2)}) async-start(f32[32,64,128]{2,1,0:T(8,128)} %get-tuple-element.25), calls=%async_computation.1 | async-start | bytes 2097152 | tf_op jit(solution)/shard_map/all_to_all | solution.py:404
  52.7 9.7 %collective-permute-start = (f32[256,128]{1,0:T(8,128)S(1)}, f32[256,128]{1,0:T(8,128)S(1)}, u32[]{:S(2)}, u32[]{:S(2)}) collective-permute-start(f32[256,128]{1,0:T(8,128)S(1)} %get-tuple-element.26), channel_id=1, source_target_pairs={{0,2},{1,3},{2,4},{3,5},{4,6},{5,7},{6,8},{7,9},{8,10},{9,11},{10,... | collective-permute-start | bytes 393224 | tf_op jit(solution)/shard_map/ppermute | solution.py:409
  54.6 9.7 %collective-permute-start.2 = (f32[256,128]{1,0:T(8,128)S(1)}, f32[256,128]{1,0:T(8,128)S(1)}, u32[]{:S(2)}, u32[]{:S(2)}) collective-permute-start(f32[256,128]{1,0:T(8,128)S(1)} %get-tuple-element.26), channel_id=1, source_target_pairs={{0,14},{1,15},{2,0},{3,1},{4,2},{5,3},{6,4},{7,5},{8,6},{9,7},{10,... | collective-permute-start | bytes 393224 | tf_op jit(solution)/shard_map/ppermute | solution.py:409
  59.2 38.7 %collective-permute-start.5 = (f32[256,128]{1,0:T(8,128)S(1)}, f32[256,128]{1,0:T(8,128)S(1)}, u32[]{:S(2)}, u32[]{:S(2)}) collective-permute-start(f32[256,128]{1,0:T(8,128)S(1)} %get-tuple-element.26), channel_id=1, source_target_pairs={{0,8},{1,9},{2,10},{3,11},{4,12},{5,13},{6,14},{7,15},{8,0},{9,1},... | collective-permute-start | bytes 393224 | tf_op jit(solution)/shard_map/ppermute | solution.py:409
  62.4 10.1 %collective-permute-start.1 = (f32[256,128]{1,0:T(8,128)S(1)}, f32[256,128]{1,0:T(8,128)S(1)}, u32[]{:S(2)}, u32[]{:S(2)}) collective-permute-start(f32[256,128]{1,0:T(8,128)S(1)} %collective-permute-done), channel_id=1, source_target_pairs={{0,2},{1,3},{2,4},{3,5},{4,6},{5,7},{6,8},{7,9},{8,10},{9,11},{10,... | collective-permute-start | bytes 393224 | tf_op jit(solution)/shard_map/ppermute | solution.py:409
  64.3 8.2 %collective-permute-start.3 = (f32[256,128]{1,0:T(8,128)S(1)}, f32[256,128]{1,0:T(8,128)S(1)}, u32[]{:S(2)}, u32[]{:S(2)}) collective-permute-start(f32[256,128]{1,0:T(8,128)S(1)} %collective-permute-done.2), channel_id=1, source_target_pairs={{0,14},{1,15},{2,0},{3,1},{4,2},{5,3},{6,4},{7,5},{8,6},{9,7},{10,... | collective-permute-start | bytes 393224 | tf_op jit(solution)/shard_map/ppermute | solution.py:409
  81.3 16.6 %all-to-all-start.2 = ((f32[16,32,128]{2,1,0:T(8,128)}), f32[16,32,128]{2,1,0:T(8,128)S(1)}, u32[]{:S(2)}, u32[]{:S(2)}) async-start(f32[16,32,128]{2,1,0:T(8,128)} %get-tuple-element.29), calls=%async_computation.2 | async-start | bytes 524288 | tf_op jit(solution)/shard_map/all_to_all | solution.py:404
  85.9 11.9 %collective-permute-start.4 = (f32[256,128]{1,0:T(8,128)S(1)}, f32[256,128]{1,0:T(8,128)S(1)}, u32[]{:S(2)}, u32[]{:S(2)}) collective-permute-start(f32[256,128]{1,0:T(8,128)S(1)} %collective-permute-done.1), channel_id=1, source_target_pairs={{0,2},{1,3},{2,4},{3,5},{4,6},{5,7},{6,8},{7,9},{8,10},{9,11},{10,... | collective-permute-start | bytes 393224 | tf_op jit(solution)/shard_map/ppermute | solution.py:409
  89.2 14.3 %collective-permute-start.6 = (f32[256,128]{1,0:T(8,128)S(1)}, f32[256,128]{1,0:T(8,128)S(1)}, u32[]{:S(2)}, u32[]{:S(2)}) collective-permute-start(f32[256,128]{1,0:T(8,128)S(1)} %collective-permute-done.3), channel_id=1, source_target_pairs={{0,14},{1,15},{2,0},{3,1},{4,2},{5,3},{6,4},{7,5},{8,6},{9,7},{10,... | collective-permute-start | bytes 393224 | tf_op jit(solution)/shard_map/ppermute | solution.py:409
  98.7 14.5 %all-to-all-start.3 = ((f32[32,16,128]{2,1,0:T(8,128)}), f32[32,16,128]{2,1,0:T(8,128)S(1)}, u32[]{:S(2)}, u32[]{:S(2)}) async-start(f32[32,16,128]{2,1,0:T(8,128)} %get-tuple-element.30), calls=%async_computation.3 | async-start | bytes 524288 | tf_op jit(solution)/shard_map/all_to_all | solution.py:404
  103.6 18.5 %collective-permute-start.7 = (f32[8,256,128]{2,1,0:T(8,128)S(1)}, f32[8,256,128]{2,1,0:T(8,128)S(1)}, u32[]{:S(2)}, u32[]{:S(2)}) collective-permute-start(f32[8,256,128]{2,1,0:T(8,128)S(1)} %bitcast_dynamic-update-slice_fusion.near_ref), channel_id=1, source_target_pairs={{0,1},{1,0},{2,3},{3,2},{4,5},{5,4},{6,7},{7,6},{8,9},{9,8},{10,11... | collective-permute-start | bytes 3145736 | tf_op jit(solution)/shard_map/ppermute | solution.py:414

commit v5 on v4

--- a/solution.py
+++ b/solution.py
@@ -10,7 +10,6 @@
 BLOCK = 64
 STEP = 16
 LANES = 128
-HOPS = (0, 7, 6, 5, 4, 1, 2, 3)
 VMEM = pl.BlockSpec(memory_space=pltpu.VMEM)
 HBM = pl.BlockSpec(memory_space=pltpu.HBM)
 PARAMS = pltpu.CompilerParams(vmem_limit_bytes=48 * 1024 * 1024)
@@ -349,9 +348,8 @@
     )(gram)
 
 
-def finish_kernel(block_ref, inv_ref, got_ref, near_ref, far_ref, slab_ref, gauss_ref, trail_ref, coupling_ref, projected_ref, sketch_ref):
+def finish_kernel(block_ref, inv_ref, got_ref, own_ref, other_ref, one_ref, two_ref, three_ref, four_ref, far_ref, slab_ref, gauss_ref, trail_ref, coupling_ref, projected_ref, sketch_ref):
     cols = slab_ref.shape[0]
-    chips = near_ref.shape[0]
     inv = inv_ref[...]
     cross = jnp.concatenate(
         [
@@ -363,13 +361,23 @@
     coupling = dot(cross, inv, 1, 1)
     coupling_ref[...] = coupling
     weights = dot(coupling, inv, 1, 0)
+    chips = slab_ref.shape[1] // (2 * LANES)
     core = lax.rem(block_ref[0], 2)
     chip = lax.div(block_ref[0], 2)
-    for step, hops in enumerate(HOPS):
-        source = lax.rem(chip + hops, chips)
-        for ref, owner in ((near_ref, 2 * source + core), (far_ref, 2 * source + 1 - core)):
-            at = pl.ds(pl.multiple_of(owner * LANES, LANES), LANES)
-            projected_ref[:, at] = slab_ref[:, at] - dot(weights, ref[step], 1, 0)
+    toward = 2 * core - 1
+    blocks = [(own_ref, None, 0, core), (other_ref, None, 0, 1 - core)]
+    for steps, ref in ((1, one_ref), (2, two_ref), (3, three_ref), (4, four_ref)):
+        blocks += [(ref, 0, steps * toward, core), (ref, 1, steps * toward, 1 - core)]
+    for steps in (1, 2, 3):
+        blocks += [
+            (far_ref, 2 * steps - 2, -steps * toward, 1 - core),
+            (far_ref, 2 * steps - 1, -steps * toward, core),
+        ]
+    for ref, index, hops, owner_core in blocks:
+        owner = 2 * lax.rem(chip + hops + chips, chips) + owner_core
+        at = pl.ds(pl.multiple_of(owner * LANES, LANES), LANES)
+        value = ref[...] if index is None else ref[index]
+        projected_ref[:, at] = slab_ref[:, at] - dot(weights, value, 1, 0)
     per = LANES // cols
     trail = jnp.concatenate(
         [
@@ -382,7 +390,7 @@
     sketch_ref[...] = trail - dot(gauss_ref[...], weights, 1, 1)
 
 
-def finish(block, inv, got, near, far, slab, gauss_panel, gauss_trail):
+def finish(block, inv, got, panel, slab, gauss_panel, gauss_trail):
     count = inv.shape[0]
     cols = slab.shape[0]
     return pl.pallas_call(
@@ -392,21 +400,21 @@
             jax.ShapeDtypeStruct(slab.shape, jnp.float32),
             jax.ShapeDtypeStruct((gauss_panel.shape[0], cols), jnp.float32),
         ),
-        in_specs=[pl.BlockSpec(memory_space=pltpu.SMEM)] + [VMEM] * 7,
+        in_specs=[pl.BlockSpec(memory_space=pltpu.SMEM)] + [VMEM] * (5 + len(panel)),
         out_specs=(VMEM,) * 3,
         compiler_params=PARAMS,
         cost_estimate=cost(3),
         name="finish",
-    )(block, inv, got, near, far, slab, gauss_panel, gauss_trail)
+    )(block, inv, got, *panel, slab, gauss_panel, gauss_trail)
 
 
 def exchange(pieces, axis):
     return lax.all_to_all(pieces, axis, 0, 0, tiled=True)
 
 
-def pass_on(value, chips):
+def pass_round(value):
     n = lax.axis_size("cols")
-    return lax.ppermute(value, "cols", [(i, (i + 2 * chips) % n) for i in range(n)])
+    return lax.ppermute(value, "cols", [(i, (i + (2 if i % 2 == 0 else -2)) % n) for i in range(n)])
 
 
 def swap_cores(value):
@@ -431,24 +439,30 @@
 
     got = exchange(send, "rows")
     part, _ = lax.optimization_barrier((part, send))
-    up, down = [part], [part]
-    for _ in range(2):
-        up.append(pass_on(up[-1], 1))
-        down.append(pass_on(down[-1], -1))
-    opposite = pass_on(part, 4)
-    got, up[2], down[2] = lax.optimization_barrier((got, up[2], down[2]))
+    other = swap_cores(part)
+    one = pass_round(jnp.stack([part, other]))
+    two = pass_round(one)
+    got, two = lax.optimization_barrier((got, two))
     send, sketch, gauss_trail = row_sums(block, pivots, got, cols_dev, n_cols)
     got = exchange(send, "cols")
-    up.append(pass_on(up[2], 1))
-    down.append(pass_on(down[2], -1))
+    held, _ = lax.optimization_barrier((two, send))
+    three = pass_round(held)
+    got, three = lax.optimization_barrier((got, three))
     send, gauss_panel = col_sums(got, n_rows)
     got = exchange(send, "rows")
-    near = jnp.stack(up + [opposite] + down[1:])
-    near, _ = lax.optimization_barrier((near, send))
-    far = swap_cores(near)
+    last, _ = lax.optimization_barrier((three, send))
+    four = pass_round(last)
+    held, _ = lax.optimization_barrier((jnp.concatenate([one, two, last]), send))
+    far = swap_cores(held)
     inv = inverse_factor(got, count)
     coupling, projected, trailing_sketch = finish(
-        block, inv, got, near, far, slab, gauss_panel, gauss_trail
+        block,
+        inv,
+        got,
+        (part, other, one, two, three, four, far),
+        slab,
+        gauss_panel,
+        gauss_trail,
     )
     return (sketch, coupling.T, projected.T, trailing_sketch)
 

time: 127 us -> 126 us (level)
  starting transfers between devices: 56.8 us -> 47.8 us
  waiting for transfers between devices: 40 us -> 48.8 us
  local copies, waits for them, and re-layouts: 3.45 us -> 1.6 us
    ppermute x7 -> x4, starting transfers between devices: 22.6 us -> 12 us  [pass_round(): lax.ppermute(value, 'cols', [(i, (i + (2 if i % 2 == 0 else -2)) % n) for...]
    ppermute x7 -> x4, waiting for transfers between devices: 9 us -> 16.5 us  [pass_round(): lax.ppermute(value, 'cols', [(i, (i + (2 if i % 2 == 0 else -2)) % n) for...]
    unnamed x19 -> x8, local copies, waits for them, and re-layouts: 3.44 us -> 1.6 us
    ppermute x1 -> x2, starting transfers between devices: 3.29 us -> 4.9 us  [swap_cores(): return lax.ppermute(value, 'cols', [(i, i ^ 1) for i in range(n)])]
    ppermute x1 -> x2, waiting for transfers between devices: 0.01 us -> 1.32 us  [swap_cores(): return lax.ppermute(value, 'cols', [(i, i ^ 1) for i in range(n)])]
  transfers between devices with their start and end apart: 12 -> 10, of which waited for: 5 -> 8; matrix products, arithmetic and copies ran while one was open for 0% -> 1% of each run, Pallas kernels for 11% -> 10%
where the time goes in v5:
time: 126 us; the launch traced here: 123 us
  waiting for transfers between devices  48.8 us (39%)
  starting transfers between devices  47.8 us (38%)
  Pallas kernels  23.5 us (19%)
  local copies, waits for them, and re-layouts  1.6 us (1%)
    all_to_all x4, waiting for transfers between devices, exchange(): return lax.all_to_all(pieces, axis, 0, 0, tiled=True)  31 us
    all_to_all x4, starting transfers between devices, exchange(): return lax.all_to_all(pieces, axis, 0, 0, tiled=True)  30.9 us
    ppermute x4, waiting for transfers between devices, pass_round(): lax.ppermute(value, 'cols', [(i, (i + (2 if i % 2 == 0 else -2)) % n) for...  16.5 us
    ppermute x4, starting transfers between devices, pass_round(): lax.ppermute(value, 'cols', [(i, (i + (2 if i % 2 == 0 else -2)) % n) for...  12 us
    pallas_call x1, Pallas kernels, inverse_factor(): pl.pallas_call(inverse_kernel, out_shape=jax.ShapeDtypeStruct((n, n), jnp...  8.86 us
    ppermute x2, starting transfers between devices, swap_cores(): return lax.ppermute(value, 'cols', [(i, i ^ 1) for i in range(n)])  4.9 us
    pallas_call x1, Pallas kernels, pick_columns(): pl.pallas_call(pick_kernel, out_shape=jax.ShapeDtypeStruct((rows_dev // L...  3.65 us
    pallas_call x1, Pallas kernels, sketch_sums(): pl.pallas_call(sketch_kernel, out_shape=jax.ShapeDtypeStruct((pieces, 24,...  3.52 us
  transfers between devices with their start and end apart: 10, of which 8 were waited for; matrix products, arithmetic and copies ran while one was open for 1% of the time, Pallas kernels for 10%

profile of v5, /device:TPU:1, one launch (start us, length us, event | category | flops | bytes accessed | tf_op | source)
XLA Modules:
  0.0 123.4 jit_solution(15114036922698991537)
XLA Ops:
  0.6 0.0 copy-start
  0.6 0.0 copy-start.2
  0.7 3.7 %pick_columns.1 = f32[16,96,128]{2,1,0:T(8,128)} custom-call(s32[1]{0:T(128)} %bitcast.block_ref, s32[1,256]{1,0:T(1,128)} %bitcast.12, f32[2048,256]{1,0:T(8,128)} %matrix_ref.1, f32[32,2048]{1,0:T(8,128)} %bitcast.9), custom_call_target="tpu_custom_call" | custom-call | flops 2000000000 | tf_op jit(solution)/shard_map/pick_columns/pallas_call | solution.py:116
  4.3 10.3 %all-to-all-start = ((f32[16,96,128]{2,1,0:T(8,128)}), f32[16,96,128]{2,1,0:T(8,128)S(1)}, u32[]{:S(2)}, u32[]{:S(2)}) async-start(f32[16,96,128]{2,1,0:T(8,128)} %pick_columns.1), calls=%async_computation | async-start | bytes 1572864 | tf_op jit(solution)/shard_map/all_to_all | solution.py:412
  14.6 0.0 copy-done
  14.6 0.0 copy-done.2
  14.6 0.0 copy-start.1
  14.6 1.6 %copy-done.1 = f32[256,2048]{1,0:T(8,128)S(1)} copy-done((f32[256,2048]{1,0:T(8,128)S(1)}, f32[256,2048]{1,0:T(8,128)}, u32[]{:S(2)}) %copy-start.1) | copy-done | bytes 2097176
  16.2 0.0 copy-start.3
  16.2 3.5 %sketch_sums.1.sketch_ref = f32[32,24,128]{2,1,0:T(8,128)S(1)} custom-call(f32[256,2048]{1,0:T(8,128)S(1)} %copy-done.1, f32[2048,256]{1,0:T(8,128)S(1)} %copy-done, f32[32,2048]{1,0:T(8,128)S(1)} %bitcast.10), custom_call_target="tpu_custom_call" | custom-call | flops 4000000000 | tf_op jit(solution)/shard_map/sketch_sums/pallas_call | solution.py:156
  19.7 17.6 %all-to-all-done.spread_ref = f32[16,96,128]{2,1,0:T(8,128)S(1)} async-done(((f32[16,96,128]{2,1,0:T(8,128)}), f32[16,96,128]{2,1,0:T(8,128)S(1)}, u32[]{:S(2)}, u32[]{:S(2)}) %all-to-all-start) | async-done | bytes 786464 | tf_op jit(solution)/shard_map/all_to_all | solution.py:412
  37.3 0.0 copy-done.3
  37.3 3.2 %part_products.1 = (f32[256,128]{1,0:T(8,128)S(1)}, f32[32,64,128]{2,1,0:T(8,128)}) custom-call(s32[1,256]{1,0:T(1,128)S(1)} %bitcast.13, f32[16,96,128]{2,1,0:T(8,128)S(1)} %all-to-all-done.spread_ref, f32[32,24,128]{2,1,0:T(8,128)S(1)} %sketch_sums.1.sketch_ref), custom_call_target="tpu_custom_call" | custom-call | flops 3000000000 | tf_op jit(solution)/shard_map/part_products/pallas_call | solution.py:203
  40.5 11.2 %all-to-all-start.1 = ((f32[32,64,128]{2,1,0:T(8,128)}), f32[32,64,128]{2,1,0:T(8,128)S(1)}, u32[]{:S(2)}, u32[]{:S(2)}) async-start(f32[32,64,128]{2,1,0:T(8,128)} %get-tuple-element.28), calls=%async_computation.1 | async-start | bytes 2097152 | tf_op jit(solution)/shard_map/all_to_all | solution.py:412
  51.7 1.9 %collective-permute-start = (f32[256,128]{1,0:T(8,128)S(1)}, f32[256,128]{1,0:T(8,128)S(1)}, u32[]{:S(2)}, u32[]{:S(2)}) collective-permute-start(f32[256,128]{1,0:T(8,128)S(1)} %get-tuple-element.29.own_ref), channel_id=1, source_target_pairs={{0,1},{1,0},{2,3},{3,2},{4,5},{5,4},{6,7},{7,6},{8,9},{9,8},{10,11... | collective-permute-start | bytes 393224 | tf_op jit(solution)/shard_map/ppermute | solution.py:422
  53.6 1.3 %collective-permute-done.other_ref = f32[256,128]{1,0:T(8,128)S(1)} collective-permute-done((f32[256,128]{1,0:T(8,128)S(1)}, f32[256,128]{1,0:T(8,128)S(1)}, u32[]{:S(2)}, u32[]{:S(2)}) %collective-permute-start) | collective-permute-done | bytes 131104 | tf_op jit(solution)/shard_map/ppermute | solution.py:422
  54.9 1.9 %collective-permute-start.1 = (f32[2,256,128]{2,1,0:T(8,128)S(1)}, f32[2,256,128]{2,1,0:T(8,128)S(1)}, u32[]{:S(2)}, u32[]{:S(2)}) collective-permute-start(f32[2,256,128]{2,1,0:T(8,128)S(1)} %pad_maximum_fusion.1), channel_id=1, source_target_pairs={{0,2},{1,15},{2,4},{3,1},{4,6},{5,3},{6,8},{7,5},{8,10},{9,7},{10,... | collective-permute-start | bytes 786440 | tf_op jit(solution)/shard_map/ppermute | solution.py:417
  56.9 5.5 %collective-permute-done.1.one_ref = f32[2,256,128]{2,1,0:T(8,128)S(1)} collective-permute-done((f32[2,256,128]{2,1,0:T(8,128)S(1)}, f32[2,256,128]{2,1,0:T(8,128)S(1)}, u32[]{:S(2)}, u32[]{:S(2)}) %collective-permute-start.1) | collective-permute-done | bytes 262176 | tf_op jit(solution)/shard_map/ppermute | solution.py:417
  62.4 3.1 %collective-permute-start.2 = (f32[2,256,128]{2,1,0:T(8,128)S(1)}, f32[2,256,128]{2,1,0:T(8,128)S(1)}, u32[]{:S(2)}, u32[]{:S(2)}) collective-permute-start(f32[2,256,128]{2,1,0:T(8,128)S(1)} %collective-permute-done.1.one_ref), channel_id=1, source_target_pairs={{0,2},{1,15},{2,4},{3,1},{4,6},{5,3},{6,8},{7,5},{8,10},{9,7},{10,... | collective-permute-start | bytes 786440 | tf_op jit(solution)/shard_map/ppermute | solution.py:417
  65.5 4.3 %collective-permute-done.2.two_ref = f32[2,256,128]{2,1,0:T(8,128)S(1)} collective-permute-done((f32[2,256,128]{2,1,0:T(8,128)S(1)}, f32[2,256,128]{2,1,0:T(8,128)S(1)}, u32[]{:S(2)}, u32[]{:S(2)}) %collective-permute-start.2) | collective-permute-done | bytes 262176 | tf_op jit(solution)/shard_map/ppermute | solution.py:417
  69.8 9.7 %all-to-all-done.1.got_ref = f32[32,64,128]{2,1,0:T(8,128)S(1)} async-done(((f32[32,64,128]{2,1,0:T(8,128)}), f32[32,64,128]{2,1,0:T(8,128)S(1)}, u32[]{:S(2)}, u32[]{:S(2)}) %all-to-all-start.1) | async-done | bytes 1048608 | tf_op jit(solution)/shard_map/all_to_all | solution.py:412
  79.4 0.9 row_sums.1
  80.3 4.6 %all-to-all-start.2 = ((f32[16,32,128]{2,1,0:T(8,128)}), f32[16,32,128]{2,1,0:T(8,128)S(1)}, u32[]{:S(2)}, u32[]{:S(2)}) async-start(f32[16,32,128]{2,1,0:T(8,128)} %get-tuple-element.32), calls=%async_computation.2 | async-start | bytes 524288 | tf_op jit(solution)/shard_map/all_to_all | solution.py:412
  84.9 4.5 %collective-permute-start.3 = (f32[2,256,128]{2,1,0:T(8,128)S(1)}, f32[2,256,128]{2,1,0:T(8,128)S(1)}, u32[]{:S(2)}, u32[]{:S(2)}) collective-permute-start(f32[2,256,128]{2,1,0:T(8,128)S(1)} %collective-permute-done.2.two_ref), channel_id=1, source_target_pairs={{0,2},{1,15},{2,4},{3,1},{4,6},{5,3},{6,8},{7,5},{8,10},{9,7},{10,... | collective-permute-start | bytes 786440 | tf_op jit(solution)/shard_map/ppermute | solution.py:417
  89.4 6.8 %collective-permute-done.3.three_ref = f32[2,256,128]{2,1,0:T(8,128)S(1)} collective-permute-done((f32[2,256,128]{2,1,0:T(8,128)S(1)}, f32[2,256,128]{2,1,0:T(8,128)S(1)}, u32[]{:S(2)}, u32[]{:S(2)}) %collective-permute-start.3) | collective-permute-done | bytes 262176 | tf_op jit(solution)/shard_map/ppermute | solution.py:417
  96.2 0.5 all-to-all-done.2.got_ref
  96.7 0.7 col_sums.1
  97.4 4.8 %all-to-all-start.3 = ((f32[32,16,128]{2,1,0:T(8,128)}), f32[32,16,128]{2,1,0:T(8,128)S(1)}, u32[]{:S(2)}, u32[]{:S(2)}) async-start(f32[32,16,128]{2,1,0:T(8,128)} %get-tuple-element.36), calls=%async_computation.3 | async-start | bytes 524288 | tf_op jit(solution)/shard_map/all_to_all | solution.py:412
  102.2 2.4 %collective-permute-start.4 = (f32[2,256,128]{2,1,0:T(8,128)S(1)}, f32[2,256,128]{2,1,0:T(8,128)S(1)}, u32[]{:S(2)}, u32[]{:S(2)}) collective-permute-start(f32[2,256,128]{2,1,0:T(8,128)S(1)} %collective-permute-done.3.three_ref), channel_id=1, source_target_pairs={{0,2},{1,15},{2,4},{3,1},{4,6},{5,3},{6,8},{7,5},{8,10},{9,7},{10,... | collective-permute-start | bytes 786440 | tf_op jit(solution)/shard_map/ppermute | solution.py:417
  104.7 0.9 pad_maximum_fusion
  105.6 3.0 %collective-permute-start.5 = (f32[6,256,128]{2,1,0:T(8,128)}, f32[6,256,128]{2,1,0:T(8,128)S(1)}, u32[]{:S(2)}, u32[]{:S(2)}) collective-permute-start(f32[6,256,128]{2,1,0:T(8,128)} %pad_maximum_fusion), channel_id=1, source_target_pairs={{0,1},{1,0},{2,3},{3,2},{4,5},{5,4},{6,7},{7,6},{8,9},{9,8},{10,11... | collective-permute-start | bytes 2359304 | tf_op jit(solution)/shard_map/ppermute | solution.py:422
  108.6 3.3 %all-to-all-done.3.gram_ref.got_ref = f32[32,16,128]{2,1,0:T(8,128)S(1)} async-done(((f32[32,16,128]{2,1,0:T(8,128)}), f32[32,16,128]{2,1,0:T(8,128)S(1)}, u32[]{:S(2)}, u32[]{:S(2)}) %all-to-all-start.3) | async-done | bytes 262176 | tf_op jit(solution)/shard_map/all_to_all | solution.py:412
  111.9 8.9 %inverse_factor.1.inv_ref = f32[256,256]{1,0:T(8,128)S(1)} custom-call(f32[32,16,128]{2,1,0:T(8,128)S(1)} %all-to-all-done.3.gram_ref.got_ref), custom_call_target="tpu_custom_call" | custom-call | flops 10000000000 | tf_op jit(solution)/shard_map/inverse_factor/pallas_call | solution.py:339
  120.8 0.0 collective-permute-done.4.four_ref
  120.8 0.0 collective-permute-done.5.far_ref
  120.8 2.6 %finish.1 = (f32[32,256]{1,0:T(8,128)}, f32[32,2048]{1,0:T(8,128)}, f32[8,32]{1,0:T(8,128)}) custom-call(s32[1]{0:T(128)} %bitcast.block_ref, f32[256,256]{1,0:T(8,128)S(1)} %inverse_factor.1.inv_ref, f32[32,16,128]{2,1,0:T(8,128)S(1)} %all-to-all-done.3.gram_ref.got_ref, f32[256,128]{1,0:T(8,128)S(1)} %get-tuple-element.29.own_ref, ...), custom_call_target="tpu_custom_call" | custom-call | flops 3000000000 | tf_op jit(solution)/shard_map/finish/pallas_call | solution.py:396
  (1 shorter events, 0.0 us)
Async XLA Ops:
  0.6 14.0 %copy-start = (f32[2048,256]{1,0:T(8,128)S(1)}, f32[2048,256]{1,0:T(8,128)}, u32[]{:S(2)}) copy-start(f32[2048,256]{1,0:T(8,128)} %matrix_ref.1) | copy-start | bytes 6291460
  0.6 14.0 %copy-start.2 = (f32[2048,32]{0,1:T(8,128)S(1)}, f32[2048,32]{0,1:T(8,128)}, u32[]{:S(2)}) copy-start(f32[2048,32]{0,1:T(8,128)} %param.7) | copy-start | bytes 786436
  4.3 33.0 %all-to-all-start = ((f32[16,96,128]{2,1,0:T(8,128)}), f32[16,96,128]{2,1,0:T(8,128)S(1)}, u32[]{:S(2)}, u32[]{:S(2)}) async-start(f32[16,96,128]{2,1,0:T(8,128)} %pick_columns.1), calls=%async_computation | async-start | bytes 1572864 | tf_op jit(solution)/shard_map/all_to_all | solution.py:412
  14.6 1.6 %copy-start.1 = (f32[256,2048]{1,0:T(8,128)S(1)}, f32[256,2048]{1,0:T(8,128)}, u32[]{:S(2)}) copy-start(f32[256,2048]{1,0:T(8,128)} %gaussian_ref) | copy-start | bytes 6291460
  16.2 21.1 %copy-start.3 = (s32[256]{0:T(256)S(1)}, s32[256]{0:T(256)}, u32[]{:S(2)}) copy-start(s32[256]{0:T(256)} %param.6) | copy-start | bytes 3076
  40.5 38.9 %all-to-all-start.1 = ((f32[32,64,128]{2,1,0:T(8,128)}), f32[32,64,128]{2,1,0:T(8,128)S(1)}, u32[]{:S(2)}, u32[]{:S(2)}) async-start(f32[32,64,128]{2,1,0:T(8,128)} %get-tuple-element.28), calls=%async_computation.1 | async-start | bytes 2097152 | tf_op jit(solution)/shard_map/all_to_all | solution.py:412
  51.7 3.2 %collective-permute-start = (f32[256,128]{1,0:T(8,128)S(1)}, f32[256,128]{1,0:T(8,128)S(1)}, u32[]{:S(2)}, u32[]{:S(2)}) collective-permute-start(f32[256,128]{1,0:T(8,128)S(1)} %get-tuple-element.29.own_ref), channel_id=1, source_target_pairs={{0,1},{1,0},{2,3},{3,2},{4,5},{5,4},{6,7},{7,6},{8,9},{9,8},{10,11... | collective-permute-start | bytes 393224 | tf_op jit(solution)/shard_map/ppermute | solution.py:422
  54.9 7.4 %collective-permute-start.1 = (f32[2,256,128]{2,1,0:T(8,128)S(1)}, f32[2,256,128]{2,1,0:T(8,128)S(1)}, u32[]{:S(2)}, u32[]{:S(2)}) collective-permute-start(f32[2,256,128]{2,1,0:T(8,128)S(1)} %pad_maximum_fusion.1), channel_id=1, source_target_pairs={{0,2},{1,15},{2,4},{3,1},{4,6},{5,3},{6,8},{7,5},{8,10},{9,7},{10,... | collective-permute-start | bytes 786440 | tf_op jit(solution)/shard_map/ppermute | solution.py:417
  62.4 7.4 %collective-permute-start.2 = (f32[2,256,128]{2,1,0:T(8,128)S(1)}, f32[2,256,128]{2,1,0:T(8,128)S(1)}, u32[]{:S(2)}, u32[]{:S(2)}) collective-permute-start(f32[2,256,128]{2,1,0:T(8,128)S(1)} %collective-permute-done.1.one_ref), channel_id=1, source_target_pairs={{0,2},{1,15},{2,4},{3,1},{4,6},{5,3},{6,8},{7,5},{8,10},{9,7},{10,... | collective-permute-start | bytes 786440 | tf_op jit(solution)/shard_map/ppermute | solution.py:417
  80.3 16.3 %all-to-all-start.2 = ((f32[16,32,128]{2,1,0:T(8,128)}), f32[16,32,128]{2,1,0:T(8,128)S(1)}, u32[]{:S(2)}, u32[]{:S(2)}) async-start(f32[16,32,128]{2,1,0:T(8,128)} %get-tuple-element.32), calls=%async_computation.2 | async-start | bytes 524288 | tf_op jit(solution)/shard_map/all_to_all | solution.py:412
  84.9 11.3 %collective-permute-start.3 = (f32[2,256,128]{2,1,0:T(8,128)S(1)}, f32[2,256,128]{2,1,0:T(8,128)S(1)}, u32[]{:S(2)}, u32[]{:S(2)}) collective-permute-start(f32[2,256,128]{2,1,0:T(8,128)S(1)} %collective-permute-done.2.two_ref), channel_id=1, source_target_pairs={{0,2},{1,15},{2,4},{3,1},{4,6},{5,3},{6,8},{7,5},{8,10},{9,7},{10,... | collective-permute-start | bytes 786440 | tf_op jit(solution)/shard_map/ppermute | solution.py:417
  97.4 14.5 %all-to-all-start.3 = ((f32[32,16,128]{2,1,0:T(8,128)}), f32[32,16,128]{2,1,0:T(8,128)S(1)}, u32[]{:S(2)}, u32[]{:S(2)}) async-start(f32[32,16,128]{2,1,0:T(8,128)} %get-tuple-element.36), calls=%async_computation.3 | async-start | bytes 524288 | tf_op jit(solution)/shard_map/all_to_all | solution.py:412
  102.2 18.5 %collective-permute-start.4 = (f32[2,256,128]{2,1,0:T(8,128)S(1)}, f32[2,256,128]{2,1,0:T(8,128)S(1)}, u32[]{:S(2)}, u32[]{:S(2)}) collective-permute-start(f32[2,256,128]{2,1,0:T(8,128)S(1)} %collective-permute-done.3.three_ref), channel_id=1, source_target_pairs={{0,2},{1,15},{2,4},{3,1},{4,6},{5,3},{6,8},{7,5},{8,10},{9,7},{10,... | collective-permute-start | bytes 786440 | tf_op jit(solution)/shard_map/ppermute | solution.py:417
  105.6 15.2 %collective-permute-start.5 = (f32[6,256,128]{2,1,0:T(8,128)}, f32[6,256,128]{2,1,0:T(8,128)S(1)}, u32[]{:S(2)}, u32[]{:S(2)}) collective-permute-start(f32[6,256,128]{2,1,0:T(8,128)} %pad_maximum_fusion), channel_id=1, source_target_pairs={{0,1},{1,0},{2,3},{3,2},{4,5},{5,4},{6,7},{7,6},{8,9},{9,8},{10,11... | collective-permute-start | bytes 2359304 | tf_op jit(solution)/shard_map/ppermute | solution.py:422

commit v6 on v5

--- a/solution.py
+++ b/solution.py
@@ -182,8 +182,9 @@
     part = hot_dot(place, spread, 1, 0)
     part_ref[...] = part
     gram_ref[...] = dot(part, part, 1, 1)
-    cross_ref[0] = dot(slab, part[:half], 1, 1)
-    cross_ref[1] = dot(slab, part[half:], 1, 1)
+    cross = dot(slab, part, 1, 1)
+    cross_ref[0] = cross[:, :half]
+    cross_ref[1] = cross[:, half:]
     send_ref[:, 0:16, :] = sketch_ref[:, 0:16, :]
     send_ref[:, 28:32, :] = sketch_ref[:, 16:20, :]
     for piece in range(pieces):
@@ -365,19 +366,18 @@
     core = lax.rem(block_ref[0], 2)
     chip = lax.div(block_ref[0], 2)
     toward = 2 * core - 1
-    blocks = [(own_ref, None, 0, core), (other_ref, None, 0, 1 - core)]
+    pairs = [((own_ref[...], other_ref[...]), 0, core)]
     for steps, ref in ((1, one_ref), (2, two_ref), (3, three_ref), (4, four_ref)):
-        blocks += [(ref, 0, steps * toward, core), (ref, 1, steps * toward, 1 - core)]
+        pairs.append(((ref[0], ref[1]), steps * toward, core))
     for steps in (1, 2, 3):
-        blocks += [
-            (far_ref, 2 * steps - 2, -steps * toward, 1 - core),
-            (far_ref, 2 * steps - 1, -steps * toward, core),
-        ]
-    for ref, index, hops, owner_core in blocks:
-        owner = 2 * lax.rem(chip + hops + chips, chips) + owner_core
-        at = pl.ds(pl.multiple_of(owner * LANES, LANES), LANES)
-        value = ref[...] if index is None else ref[index]
-        projected_ref[:, at] = slab_ref[:, at] - dot(weights, value, 1, 0)
+        pairs.append(((far_ref[2 * steps - 2], far_ref[2 * steps - 1]), -steps * toward, 1 - core))
+    for values, hops, first_core in pairs:
+        taken = dot(weights, jnp.concatenate(values, axis=1), 1, 0)
+        source = 2 * lax.rem(chip + hops + chips, chips)
+        for half, owner in enumerate((source + first_core, source + 1 - first_core)):
+            at = pl.ds(pl.multiple_of(owner * LANES, LANES), LANES)
+            part = taken[:, half * LANES : (half + 1) * LANES]
+            projected_ref[:, at] = slab_ref[:, at] - part
     per = LANES // cols
     trail = jnp.concatenate(
         [

time: 126 us -> 125 us (level)
  no operation moved by 1% of the time
where the time goes in v6:
time: 125 us; the launch traced here: 123 us
  waiting for transfers between devices  48.8 us (39%)
  starting transfers between devices  47.8 us (38%)
  Pallas kernels  23.3 us (19%)
  local copies, waits for them, and re-layouts  1.6 us (1%)
    all_to_all x4, waiting for transfers between devices, exchange(): return lax.all_to_all(pieces, axis, 0, 0, tiled=True)  31 us
    all_to_all x4, starting transfers between devices, exchange(): return lax.all_to_all(pieces, axis, 0, 0, tiled=True)  30.9 us
    ppermute x4, waiting for transfers between devices, pass_round(): lax.ppermute(value, 'cols', [(i, (i + (2 if i % 2 == 0 else -2)) % n) for...  16.5 us
    ppermute x4, starting transfers between devices, pass_round(): lax.ppermute(value, 'cols', [(i, (i + (2 if i % 2 == 0 else -2)) % n) for...  12 us
    pallas_call x1, Pallas kernels, inverse_factor(): pl.pallas_call(inverse_kernel, out_shape=jax.ShapeDtypeStruct((n, n), jnp...  8.86 us
    ppermute x2, starting transfers between devices, swap_cores(): return lax.ppermute(value, 'cols', [(i, i ^ 1) for i in range(n)])  4.9 us
    pallas_call x1, Pallas kernels, pick_columns(): pl.pallas_call(pick_kernel, out_shape=jax.ShapeDtypeStruct((rows_dev // L...  3.65 us
    pallas_call x1, Pallas kernels, sketch_sums(): pl.pallas_call(sketch_kernel, out_shape=jax.ShapeDtypeStruct((pieces, 24,...  3.52 us
  transfers between devices with their start and end apart: 10, of which 8 were waited for; matrix products, arithmetic and copies ran while one was open for 1% of the time, Pallas kernels for 10%

profile of v6, /device:TPU:1, one launch (start us, length us, event | category | flops | bytes accessed | tf_op | source)
XLA Modules:
  0.0 123.2 jit_solution(17191753669324541860)
XLA Ops:
  0.6 0.0 copy-start
  0.6 0.0 copy-start.2
  0.7 3.7 %pick_columns.1 = f32[16,96,128]{2,1,0:T(8,128)} custom-call(s32[1]{0:T(128)} %bitcast.block_ref, s32[1,256]{1,0:T(1,128)} %bitcast.12, f32[2048,256]{1,0:T(8,128)} %matrix_ref.1, f32[32,2048]{1,0:T(8,128)} %bitcast.9), custom_call_target="tpu_custom_call" | custom-call | flops 2000000000 | tf_op jit(solution)/shard_map/pick_columns/pallas_call | solution.py:116
  4.3 10.3 %all-to-all-start = ((f32[16,96,128]{2,1,0:T(8,128)}), f32[16,96,128]{2,1,0:T(8,128)S(1)}, u32[]{:S(2)}, u32[]{:S(2)}) async-start(f32[16,96,128]{2,1,0:T(8,128)} %pick_columns.1), calls=%async_computation | async-start | bytes 1572864 | tf_op jit(solution)/shard_map/all_to_all | solution.py:412
  14.6 0.0 copy-done
  14.6 0.0 copy-done.2
  14.6 0.0 copy-start.1
  14.6 1.6 %copy-done.1 = f32[256,2048]{1,0:T(8,128)S(1)} copy-done((f32[256,2048]{1,0:T(8,128)S(1)}, f32[256,2048]{1,0:T(8,128)}, u32[]{:S(2)}) %copy-start.1) | copy-done | bytes 2097176
  16.2 0.0 copy-start.3
  16.2 3.5 %sketch_sums.1.sketch_ref = f32[32,24,128]{2,1,0:T(8,128)S(1)} custom-call(f32[256,2048]{1,0:T(8,128)S(1)} %copy-done.1, f32[2048,256]{1,0:T(8,128)S(1)} %copy-done, f32[32,2048]{1,0:T(8,128)S(1)} %bitcast.10), custom_call_target="tpu_custom_call" | custom-call | flops 4000000000 | tf_op jit(solution)/shard_map/sketch_sums/pallas_call | solution.py:156
  19.7 17.6 %all-to-all-done.spread_ref = f32[16,96,128]{2,1,0:T(8,128)S(1)} async-done(((f32[16,96,128]{2,1,0:T(8,128)}), f32[16,96,128]{2,1,0:T(8,128)S(1)}, u32[]{:S(2)}, u32[]{:S(2)}) %all-to-all-start) | async-done | bytes 786464 | tf_op jit(solution)/shard_map/all_to_all | solution.py:412
  37.3 0.0 copy-done.3
  37.3 3.0 %part_products.1 = (f32[256,128]{1,0:T(8,128)S(1)}, f32[32,64,128]{2,1,0:T(8,128)}) custom-call(s32[1,256]{1,0:T(1,128)S(1)} %bitcast.13, f32[16,96,128]{2,1,0:T(8,128)S(1)} %all-to-all-done.spread_ref, f32[32,24,128]{2,1,0:T(8,128)S(1)} %sketch_sums.1.sketch_ref), custom_call_target="tpu_custom_call" | custom-call | flops 3000000000 | tf_op jit(solution)/shard_map/part_products/pallas_call | solution.py:204
  40.3 11.2 %all-to-all-start.1 = ((f32[32,64,128]{2,1,0:T(8,128)}), f32[32,64,128]{2,1,0:T(8,128)S(1)}, u32[]{:S(2)}, u32[]{:S(2)}) async-start(f32[32,64,128]{2,1,0:T(8,128)} %get-tuple-element.28), calls=%async_computation.1 | async-start | bytes 2097152 | tf_op jit(solution)/shard_map/all_to_all | solution.py:412
  51.5 1.9 %collective-permute-start = (f32[256,128]{1,0:T(8,128)S(1)}, f32[256,128]{1,0:T(8,128)S(1)}, u32[]{:S(2)}, u32[]{:S(2)}) collective-permute-start(f32[256,128]{1,0:T(8,128)S(1)} %get-tuple-element.29.own_ref), channel_id=1, source_target_pairs={{0,1},{1,0},{2,3},{3,2},{4,5},{5,4},{6,7},{7,6},{8,9},{9,8},{10,11... | collective-permute-start | bytes 393224 | tf_op jit(solution)/shard_map/ppermute | solution.py:422
  53.4 1.3 %collective-permute-done.other_ref = f32[256,128]{1,0:T(8,128)S(1)} collective-permute-done((f32[256,128]{1,0:T(8,128)S(1)}, f32[256,128]{1,0:T(8,128)S(1)}, u32[]{:S(2)}, u32[]{:S(2)}) %collective-permute-start) | collective-permute-done | bytes 131104 | tf_op jit(solution)/shard_map/ppermute | solution.py:422
  54.8 1.9 %collective-permute-start.1 = (f32[2,256,128]{2,1,0:T(8,128)S(1)}, f32[2,256,128]{2,1,0:T(8,128)S(1)}, u32[]{:S(2)}, u32[]{:S(2)}) collective-permute-start(f32[2,256,128]{2,1,0:T(8,128)S(1)} %pad_maximum_fusion.1), channel_id=1, source_target_pairs={{0,2},{1,15},{2,4},{3,1},{4,6},{5,3},{6,8},{7,5},{8,10},{9,7},{10,... | collective-permute-start | bytes 786440 | tf_op jit(solution)/shard_map/ppermute | solution.py:417
  56.7 5.5 %collective-permute-done.1.one_ref = f32[2,256,128]{2,1,0:T(8,128)S(1)} collective-permute-done((f32[2,256,128]{2,1,0:T(8,128)S(1)}, f32[2,256,128]{2,1,0:T(8,128)S(1)}, u32[]{:S(2)}, u32[]{:S(2)}) %collective-permute-start.1) | collective-permute-done | bytes 262176 | tf_op jit(solution)/shard_map/ppermute | solution.py:417
  62.2 3.1 %collective-permute-start.2 = (f32[2,256,128]{2,1,0:T(8,128)S(1)}, f32[2,256,128]{2,1,0:T(8,128)S(1)}, u32[]{:S(2)}, u32[]{:S(2)}) collective-permute-start(f32[2,256,128]{2,1,0:T(8,128)S(1)} %collective-permute-done.1.one_ref), channel_id=1, source_target_pairs={{0,2},{1,15},{2,4},{3,1},{4,6},{5,3},{6,8},{7,5},{8,10},{9,7},{10,... | collective-permute-start | bytes 786440 | tf_op jit(solution)/shard_map/ppermute | solution.py:417
  65.3 4.3 %collective-permute-done.2.two_ref = f32[2,256,128]{2,1,0:T(8,128)S(1)} collective-permute-done((f32[2,256,128]{2,1,0:T(8,128)S(1)}, f32[2,256,128]{2,1,0:T(8,128)S(1)}, u32[]{:S(2)}, u32[]{:S(2)}) %collective-permute-start.2) | collective-permute-done | bytes 262176 | tf_op jit(solution)/shard_map/ppermute | solution.py:417
  69.6 9.7 %all-to-all-done.1.got_ref = f32[32,64,128]{2,1,0:T(8,128)S(1)} async-done(((f32[32,64,128]{2,1,0:T(8,128)}), f32[32,64,128]{2,1,0:T(8,128)S(1)}, u32[]{:S(2)}, u32[]{:S(2)}) %all-to-all-start.1) | async-done | bytes 1048608 | tf_op jit(solution)/shard_map/all_to_all | solution.py:412
  79.3 0.9 row_sums.1
  80.2 4.6 %all-to-all-start.2 = ((f32[16,32,128]{2,1,0:T(8,128)}), f32[16,32,128]{2,1,0:T(8,128)S(1)}, u32[]{:S(2)}, u32[]{:S(2)}) async-start(f32[16,32,128]{2,1,0:T(8,128)} %get-tuple-element.32), calls=%async_computation.2 | async-start | bytes 524288 | tf_op jit(solution)/shard_map/all_to_all | solution.py:412
  84.8 4.5 %collective-permute-start.3 = (f32[2,256,128]{2,1,0:T(8,128)S(1)}, f32[2,256,128]{2,1,0:T(8,128)S(1)}, u32[]{:S(2)}, u32[]{:S(2)}) collective-permute-start(f32[2,256,128]{2,1,0:T(8,128)S(1)} %collective-permute-done.2.two_ref), channel_id=1, source_target_pairs={{0,2},{1,15},{2,4},{3,1},{4,6},{5,3},{6,8},{7,5},{8,10},{9,7},{10,... | collective-permute-start | bytes 786440 | tf_op jit(solution)/shard_map/ppermute | solution.py:417
  89.3 6.8 %collective-permute-done.3.three_ref = f32[2,256,128]{2,1,0:T(8,128)S(1)} collective-permute-done((f32[2,256,128]{2,1,0:T(8,128)S(1)}, f32[2,256,128]{2,1,0:T(8,128)S(1)}, u32[]{:S(2)}, u32[]{:S(2)}) %collective-permute-start.3) | collective-permute-done | bytes 262176 | tf_op jit(solution)/shard_map/ppermute | solution.py:417
  96.0 0.5 all-to-all-done.2.got_ref
  96.5 0.7 col_sums.1
  97.2 4.8 %all-to-all-start.3 = ((f32[32,16,128]{2,1,0:T(8,128)}), f32[32,16,128]{2,1,0:T(8,128)S(1)}, u32[]{:S(2)}, u32[]{:S(2)}) async-start(f32[32,16,128]{2,1,0:T(8,128)} %get-tuple-element.36), calls=%async_computation.3 | async-start | bytes 524288 | tf_op jit(solution)/shard_map/all_to_all | solution.py:412
  102.1 2.4 %collective-permute-start.4 = (f32[2,256,128]{2,1,0:T(8,128)S(1)}, f32[2,256,128]{2,1,0:T(8,128)S(1)}, u32[]{:S(2)}, u32[]{:S(2)}) collective-permute-start(f32[2,256,128]{2,1,0:T(8,128)S(1)} %collective-permute-done.3.three_ref), channel_id=1, source_target_pairs={{0,2},{1,15},{2,4},{3,1},{4,6},{5,3},{6,8},{7,5},{8,10},{9,7},{10,... | collective-permute-start | bytes 786440 | tf_op jit(solution)/shard_map/ppermute | solution.py:417
  104.5 0.9 pad_maximum_fusion
  105.5 3.0 %collective-permute-start.5 = (f32[6,256,128]{2,1,0:T(8,128)}, f32[6,256,128]{2,1,0:T(8,128)S(1)}, u32[]{:S(2)}, u32[]{:S(2)}) collective-permute-start(f32[6,256,128]{2,1,0:T(8,128)} %pad_maximum_fusion), channel_id=1, source_target_pairs={{0,1},{1,0},{2,3},{3,2},{4,5},{5,4},{6,7},{7,6},{8,9},{9,8},{10,11... | collective-permute-start | bytes 2359304 | tf_op jit(solution)/shard_map/ppermute | solution.py:422
  108.5 3.3 %all-to-all-done.3.gram_ref.got_ref = f32[32,16,128]{2,1,0:T(8,128)S(1)} async-done(((f32[32,16,128]{2,1,0:T(8,128)}), f32[32,16,128]{2,1,0:T(8,128)S(1)}, u32[]{:S(2)}, u32[]{:S(2)}) %all-to-all-start.3) | async-done | bytes 262176 | tf_op jit(solution)/shard_map/all_to_all | solution.py:412
  111.7 8.9 %inverse_factor.1.inv_ref = f32[256,256]{1,0:T(8,128)S(1)} custom-call(f32[32,16,128]{2,1,0:T(8,128)S(1)} %all-to-all-done.3.gram_ref.got_ref), custom_call_target="tpu_custom_call" | custom-call | flops 10000000000 | tf_op jit(solution)/shard_map/inverse_factor/pallas_call | solution.py:340
  120.6 0.0 collective-permute-done.4.four_ref
  120.6 0.0 collective-permute-done.5.far_ref
  120.6 2.6 %finish.1 = (f32[32,256]{1,0:T(8,128)}, f32[32,2048]{1,0:T(8,128)}, f32[8,32]{1,0:T(8,128)}) custom-call(s32[1]{0:T(128)} %bitcast.block_ref, f32[256,256]{1,0:T(8,128)S(1)} %inverse_factor.1.inv_ref, f32[32,16,128]{2,1,0:T(8,128)S(1)} %all-to-all-done.3.gram_ref.got_ref, f32[256,128]{1,0:T(8,128)S(1)} %get-tuple-element.29.own_ref, ...), custom_call_target="tpu_custom_call" | custom-call | flops 3000000000 | tf_op jit(solution)/shard_map/finish/pallas_call | solution.py:396
  (1 shorter events, 0.0 us)
Async XLA Ops:
  0.6 14.0 %copy-start = (f32[2048,256]{1,0:T(8,128)S(1)}, f32[2048,256]{1,0:T(8,128)}, u32[]{:S(2)}) copy-start(f32[2048,256]{1,0:T(8,128)} %matrix_ref.1) | copy-start | bytes 6291460
  0.6 14.0 %copy-start.2 = (f32[2048,32]{0,1:T(8,128)S(1)}, f32[2048,32]{0,1:T(8,128)}, u32[]{:S(2)}) copy-start(f32[2048,32]{0,1:T(8,128)} %param.7) | copy-start | bytes 786436
  4.3 33.0 %all-to-all-start = ((f32[16,96,128]{2,1,0:T(8,128)}), f32[16,96,128]{2,1,0:T(8,128)S(1)}, u32[]{:S(2)}, u32[]{:S(2)}) async-start(f32[16,96,128]{2,1,0:T(8,128)} %pick_columns.1), calls=%async_computation | async-start | bytes 1572864 | tf_op jit(solution)/shard_map/all_to_all | solution.py:412
  14.6 1.6 %copy-start.1 = (f32[256,2048]{1,0:T(8,128)S(1)}, f32[256,2048]{1,0:T(8,128)}, u32[]{:S(2)}) copy-start(f32[256,2048]{1,0:T(8,128)} %gaussian_ref) | copy-start | bytes 6291460
  16.2 21.1 %copy-start.3 = (s32[256]{0:T(256)S(1)}, s32[256]{0:T(256)}, u32[]{:S(2)}) copy-start(s32[256]{0:T(256)} %param.6) | copy-start | bytes 3076
  40.3 38.9 %all-to-all-start.1 = ((f32[32,64,128]{2,1,0:T(8,128)}), f32[32,64,128]{2,1,0:T(8,128)S(1)}, u32[]{:S(2)}, u32[]{:S(2)}) async-start(f32[32,64,128]{2,1,0:T(8,128)} %get-tuple-element.28), calls=%async_computation.1 | async-start | bytes 2097152 | tf_op jit(solution)/shard_map/all_to_all | solution.py:412
  51.5 3.2 %collective-permute-start = (f32[256,128]{1,0:T(8,128)S(1)}, f32[256,128]{1,0:T(8,128)S(1)}, u32[]{:S(2)}, u32[]{:S(2)}) collective-permute-start(f32[256,128]{1,0:T(8,128)S(1)} %get-tuple-element.29.own_ref), channel_id=1, source_target_pairs={{0,1},{1,0},{2,3},{3,2},{4,5},{5,4},{6,7},{7,6},{8,9},{9,8},{10,11... | collective-permute-start | bytes 393224 | tf_op jit(solution)/shard_map/ppermute | solution.py:422
  54.8 7.4 %collective-permute-start.1 = (f32[2,256,128]{2,1,0:T(8,128)S(1)}, f32[2,256,128]{2,1,0:T(8,128)S(1)}, u32[]{:S(2)}, u32[]{:S(2)}) collective-permute-start(f32[2,256,128]{2,1,0:T(8,128)S(1)} %pad_maximum_fusion.1), channel_id=1, source_target_pairs={{0,2},{1,15},{2,4},{3,1},{4,6},{5,3},{6,8},{7,5},{8,10},{9,7},{10,... | collective-permute-start | bytes 786440 | tf_op jit(solution)/shard_map/ppermute | solution.py:417
  62.2 7.4 %collective-permute-start.2 = (f32[2,256,128]{2,1,0:T(8,128)S(1)}, f32[2,256,128]{2,1,0:T(8,128)S(1)}, u32[]{:S(2)}, u32[]{:S(2)}) collective-permute-start(f32[2,256,128]{2,1,0:T(8,128)S(1)} %collective-permute-done.1.one_ref), channel_id=1, source_target_pairs={{0,2},{1,15},{2,4},{3,1},{4,6},{5,3},{6,8},{7,5},{8,10},{9,7},{10,... | collective-permute-start | bytes 786440 | tf_op jit(solution)/shard_map/ppermute | solution.py:417
  80.2 16.3 %all-to-all-start.2 = ((f32[16,32,128]{2,1,0:T(8,128)}), f32[16,32,128]{2,1,0:T(8,128)S(1)}, u32[]{:S(2)}, u32[]{:S(2)}) async-start(f32[16,32,128]{2,1,0:T(8,128)} %get-tuple-element.32), calls=%async_computation.2 | async-start | bytes 524288 | tf_op jit(solution)/shard_map/all_to_all | solution.py:412
  84.8 11.3 %collective-permute-start.3 = (f32[2,256,128]{2,1,0:T(8,128)S(1)}, f32[2,256,128]{2,1,0:T(8,128)S(1)}, u32[]{:S(2)}, u32[]{:S(2)}) collective-permute-start(f32[2,256,128]{2,1,0:T(8,128)S(1)} %collective-permute-done.2.two_ref), channel_id=1, source_target_pairs={{0,2},{1,15},{2,4},{3,1},{4,6},{5,3},{6,8},{7,5},{8,10},{9,7},{10,... | collective-permute-start | bytes 786440 | tf_op jit(solution)/shard_map/ppermute | solution.py:417
  97.2 14.5 %all-to-all-start.3 = ((f32[32,16,128]{2,1,0:T(8,128)}), f32[32,16,128]{2,1,0:T(8,128)S(1)}, u32[]{:S(2)}, u32[]{:S(2)}) async-start(f32[32,16,128]{2,1,0:T(8,128)} %get-tuple-element.36), calls=%async_computation.3 | async-start | bytes 524288 | tf_op jit(solution)/shard_map/all_to_all | solution.py:412
  102.1 18.5 %collective-permute-start.4 = (f32[2,256,128]{2,1,0:T(8,128)S(1)}, f32[2,256,128]{2,1,0:T(8,128)S(1)}, u32[]{:S(2)}, u32[]{:S(2)}) collective-permute-start(f32[2,256,128]{2,1,0:T(8,128)S(1)} %collective-permute-done.3.three_ref), channel_id=1, source_target_pairs={{0,2},{1,15},{2,4},{3,1},{4,6},{5,3},{6,8},{7,5},{8,10},{9,7},{10,... | collective-permute-start | bytes 786440 | tf_op jit(solution)/shard_map/ppermute | solution.py:417
  105.5 15.2 %collective-permute-start.5 = (f32[6,256,128]{2,1,0:T(8,128)}, f32[6,256,128]{2,1,0:T(8,128)S(1)}, u32[]{:S(2)}, u32[]{:S(2)}) collective-permute-start(f32[6,256,128]{2,1,0:T(8,128)} %pad_maximum_fusion), channel_id=1, source_target_pairs={{0,1},{1,0},{2,3},{3,2},{4,5},{5,4},{6,7},{7,6},{8,9},{9,8},{10,11... | collective-permute-start | bytes 2359304 | tf_op jit(solution)/shard_map/ppermute | solution.py:422
